TPU v7x, 256 devices: a whole 4x4x8 slice. The times are simulated.
256 devices in a mesh: tm: 2 (over core), row: 4 (over x), col: 32 (over z, y).
Axes of the slice: x: 4, y: 4, z: 8, core: 2. Of those that a mesh axis runs over, the one named last changes fastest.
Arguments:
- latent: bfloat16 [8, 136, 256, 256], P('tm', 'row', 'col'), may hold values from -6 to 6
- conv_cache: bfloat16 [3, 2, 136, 256, 256], P(None, None, 'row', 'col'), may hold values from -6 to 6
- conv_weight: bfloat16 [3, 3, 3, 3, 256, 256], replicated, may hold values from -0.078125 to 0.078125
- conv_bias: float32 [3, 256], replicated, may hold values from -3 to 3
- w_query: bfloat16 [256, 256], replicated, may hold values from -16 to 16
- w_key: bfloat16 [256, 256], replicated, may hold values from -0.375 to 0.375
- w_value: bfloat16 [256, 256], replicated, may hold values from -0.375 to 0.375
- w_out: bfloat16 [256, 256], replicated, may hold values from -0.375 to 0.375
- cache_key: bfloat16 [2, 136, 256, 256], P(None, 'row', 'col'), may hold values from -6 to 6
- cache_value: bfloat16 [2, 136, 256, 256], P(None, 'row', 'col'), may hold values from -6 to 6
Outputs:
- encoded: bfloat16 [8, 136, 256, 256], P('tm', 'row', 'col')
All inputs are finite; a program needn't handle non-finite values.
Results may differ from a plain program's by a relative error of at most 0.04.
Values may be sent and summed in bfloat16 or wider, within the bound.
No kernel may reach another device: no remote copies, remote signals or barrier semaphores. Data moves between devices by JAX's collectives and lax.ppermute only.
A program may use at most 128 MiB of HBM per device.

v0:
```python
import functools

import jax
import jax.numpy as jnp
from jax import lax
from jax.experimental import pallas as pl
from jax.experimental.pallas import tpu as pltpu
from jax.sharding import PartitionSpec as P

HEADS = 8
HD = 32
C = 256
T = 8
FRAMES = 4
ROWS = 34
HALF = 17
COLS = 8
EXT = HALF + 6
BF = jnp.bfloat16
F32 = jnp.float32
TAPS = [(a, b, c) for a in range(3) for b in range(3) for c in range(3)]
LAYER_K = 27 * C

ANY = pl.BlockSpec(memory_space=pl.ANY)
VM = pl.BlockSpec(memory_space=pltpu.VMEM)


def shape(*dims, dtype=BF):
    return jax.ShapeDtypeStruct(dims, dtype)


def run_copies(copies):
    for copy in copies:
        copy.start()
    for copy in copies:
        copy.wait()


def pack_rows(latent, cache, out_a, out_b, sems):
    half = lax.axis_index("tm")
    row_a = 31 * (1 - half)
    row_b = 31 * half
    run_copies([
        pltpu.make_async_copy(latent.at[:, pl.ds(row_a, 3)], out_a.at[0:4], sems.at[0]),
        pltpu.make_async_copy(cache.at[:, pl.ds(row_a, 3)], out_a.at[4:10], sems.at[1]),
        pltpu.make_async_copy(latent.at[:, pl.ds(row_b, 3)], out_b, sems.at[2]),
    ])


def assemble(own, other, cache, halo_a, halo_b, lt, ht, left, right, stage, wide, sems):
    half = lax.axis_index("tm")
    first, second = 4 * half, 4 - 4 * half
    start, at, edge = 14 * half, 3 - 3 * half, 20 * half
    run_copies([
        pltpu.make_async_copy(
            own.at[:, pl.ds(start, 20)], stage.at[pl.ds(first, 4), pl.ds(at, 20)], sems.at[0]),
        pltpu.make_async_copy(
            other.at[:, pl.ds(start, 20)], stage.at[pl.ds(second, 4), pl.ds(at, 20)], sems.at[1]),
        pltpu.make_async_copy(
            cache.at[:, pl.ds(start, 20)], stage.at[8:14, pl.ds(at, 20)], sems.at[2]),
        pltpu.make_async_copy(
            halo_a.at[0:4], stage.at[pl.ds(first, 4), pl.ds(edge, 3)], sems.at[3]),
        pltpu.make_async_copy(halo_a.at[4:10], stage.at[8:14, pl.ds(edge, 3)], sems.at[4]),
        pltpu.make_async_copy(
            halo_b, stage.at[pl.ds(second, 4), pl.ds(edge, 3)], sems.at[5]),
    ])
    sub = lax.broadcasted_iota(jnp.int32, (T, C), 0)
    for slot in range(4):
        wide[slot, 14 * COLS:16 * COLS] = jnp.zeros((2 * COLS, 128), F32)

    def row(e, slot):
        for frame in range(14):
            v = stage[frame, e].astype(F32)
            wide[2 * slot, frame * COLS:(frame + 1) * COLS] = v[:, :128]
            wide[2 * slot + 1, frame * COLS:(frame + 1) * COLS] = v[:, 128:]
        past = []
        for col in range(COLS):
            lat = jnp.concatenate(
                [wide[2 * slot + lane, pl.ds(col, T, stride=COLS)] for lane in (0, 1)], 1)
            old = jnp.concatenate(
                [wide[2 * slot + lane, pl.ds(T * COLS + col, T, stride=COLS)]
                 for lane in (0, 1)], 1)
            lt[e, col] = lat.astype(BF)
            ht[e, col] = old.astype(BF)
            past.append(old)
            if col < 3:
                left[e, col] = lat.astype(BF)
            if col >= 5:
                right[e, col - 5] = lat.astype(BF)
        left[e, 3] = jnp.where(sub < 6, past[0], pltpu.roll(past[2], 6, 0)).astype(BF)
        left[e, 4] = past[1].astype(BF)
        right[e, 3] = jnp.where(sub < 6, past[7], pltpu.roll(past[5], 6, 0)).astype(BF)
        right[e, 4] = past[6].astype(BF)

    def pair(i, carry):
        row(2 * i, 0)
        row(2 * i + 1, 1)
        return carry

    lax.fori_loop(0, EXT // 2, pair, 0)
    row(EXT - 1, 0)


def put(dst, r, at, now, past, layer):
    n = now.shape[0]
    sub = lax.broadcasted_iota(jnp.int32, (n, T, C), 1)

    def roll(v, k):
        k %= T
        return v if k == 0 else pltpu.roll(v, k, 1)

    dst[2, r, at:at + n] = now
    dst[1, r, at:at + n] = jnp.where(sub < 1, roll(past, -2 * layer - 1), roll(now, 1))
    dst[0, r, at:at + n] = jnp.where(sub < 2, roll(past, -2 * layer), roll(now, 2))


def conv(src, rows, groups, weights, bias):
    total = None
    count = sum(n for _, n in groups)
    for a in range(3):
        for b in range(3):
            parts = []
            for c in range(3):
                cols = [src[a, b:b + rows, first + c:first + c + n] for first, n in groups]
                block = cols[0] if len(cols) == 1 else jnp.concatenate(cols, 1)
                parts.append(block.reshape(rows * count * T, C).astype(BF))
            k = (a * 3 + b) * 3 * C
            part = jnp.dot(
                jnp.concatenate(parts, 1), weights[k:k + 3 * C], preferred_element_type=F32)
            total = part if total is None else total + part
    return (total + bias).reshape(rows, count, T, C)


def silu(v):
    return v / (1.0 + jnp.exp(-v))


def row_limits(border):
    half, place = lax.axis_index("tm"), lax.axis_index("row")
    low = jnp.where((half == 0) & (place == 0), border, 0)
    high = jnp.where(
        (half == 1) & (place == lax.axis_size("row") - 1), HALF + border, HALF + 2 * border)
    return low, high


def weight_copies(weights, held, sems):
    third = LAYER_K // 3
    return [
        pltpu.make_async_copy(
            weights.at[pl.ds(i * third, third)], held.at[pl.ds(i * third, third)], sems.at[i])
        for i in range(9)
    ]


def interior(lt, ht, weights, bias, out1, out2, out3, x, y, z, res, held, sems):
    copies = weight_copies(weights, held, sems)
    for copy in copies:
        copy.start()

    def fill(r, carry):
        put(x, r, 0, lt[r].astype(F32), ht[r].astype(F32), 0)
        return carry

    lax.fori_loop(0, EXT, fill, 0)
    for copy in copies[0:3]:
        copy.wait()
    res[...] = conv(x, 21, [(0, 6)], held[0:LAYER_K], bias[0:1])
    low, high = row_limits(2)

    def one(r, carry):
        v = jnp.where((r >= low) & (r < high), silu(res[r]), 0.0).astype(BF)
        out1[r, 0:2] = v[0:2]
        out1[r, 2:4] = v[4:6]
        put(y, r, 0, v.astype(F32), ht[r + 1, 1:7].astype(F32), 1)
        return carry

    lax.fori_loop(0, 21, one, 0)
    for copy in copies[3:6]:
        copy.wait()
    res[0:19, 0:4] = conv(y, 19, [(0, 4)], held[LAYER_K:2 * LAYER_K], bias[1:2])
    low2, high2 = row_limits(1)

    def two(r, carry):
        v = jnp.where((r >= low2) & (r < high2), silu(res[r, 0:4]), 0.0).astype(BF)
        out2[r] = v
        put(z, r, 0, v.astype(F32), ht[r + 2, 2:6].astype(F32), 2)
        return carry

    lax.fori_loop(0, 19, two, 0)
    for copy in copies[6:9]:
        copy.wait()
    last = conv(z, 17, [(0, 2)], held[2 * LAYER_K:3 * LAYER_K], bias[2:3])
    out3[...] = (last + lt[3:20, 3:5].astype(F32)).astype(BF)


def exterior(lt, ht, from_left, from_right, in1, in2, in3, weights, bias, wq, wk, wv, wo,
             key_cache, value_cache, mine, theirs, x, y, z, res, held, hid, qs, ks, vs, mix,
             ck, cv, ckw, cvw, enc, sems):
    half = lax.axis_index("tm")
    copies = weight_copies(weights, held, sems)
    for copy in copies:
        copy.start()
    more = [
        pltpu.make_async_copy(key_cache.at[:, pl.ds(HALF * half, HALF)], ck, sems.at[9]),
        pltpu.make_async_copy(value_cache.at[:, pl.ds(HALF * half, HALF)], cv, sems.at[10]),
    ]
    for copy in more:
        copy.start()
    place = lax.axis_index("col")
    has_left = place > 0
    has_right = place < lax.axis_size("col") - 1
    groups = [(0, 3), (5, 3)]

    def fill(r, carry):
        for side, at, own in ((from_left, 0, 3), (from_right, 7, 5)):
            t1 = side[r, 3].astype(F32)
            t2 = side[r, 4].astype(F32)
            t3 = pltpu.roll(t1, 2, 0)
            order = (t3, t2, t1) if at == 0 else (t1, t2, t3)
            past = jnp.concatenate([v[None] for v in order], 0)
            put(x, r, at, side[r, 0:3].astype(F32), past, 0)
        put(x, r, 3, lt[r, 0:2].astype(F32), ht[r, 0:2].astype(F32), 0)
        put(x, r, 5, lt[r, 6:8].astype(F32), ht[r, 6:8].astype(F32), 0)
        return carry

    lax.fori_loop(0, EXT, fill, 0)
    for copy in copies[0:3]:
        copy.wait()
    res[...] = conv(x, 21, groups, held[0:LAYER_K], bias[0:1])
    low, high = row_limits(2)

    def one(r, carry):
        ok = (r >= low) & (r < high)
        v = silu(res[r]).astype(BF).astype(F32)
        zero = jnp.zeros((1, T, C), F32)
        l = [jnp.where(ok & has_left, v[0:2], 0.0), jnp.where(ok, v[2:3], zero)]
        g = [jnp.where(ok, v[3:4], zero), jnp.where(ok & has_right, v[4:6], 0.0)]
        e = r + 1
        put(y, r, 0, jnp.concatenate(l + [in1[r, 0:2].astype(F32)], 0), jnp.concatenate(
            [from_left[e, 4:5].astype(F32), from_left[e, 3:4].astype(F32),
             ht[e, 0:3].astype(F32)], 0), 1)
        put(y, r, 5, jnp.concatenate([in1[r, 2:4].astype(F32)] + g, 0), jnp.concatenate(
            [ht[e, 5:8].astype(F32), from_right[e, 3:4].astype(F32),
             from_right[e, 4:5].astype(F32)], 0), 1)
        return carry

    lax.fori_loop(0, 21, one, 0)
    for copy in copies[3:6]:
        copy.wait()
    res[0:19] = conv(y, 19, groups, held[LAYER_K:2 * LAYER_K], bias[1:2])
    low2, high2 = row_limits(1)

    def two(r, carry):
        ok = (r >= low2) & (r < high2)
        v = silu(res[r]).astype(BF).astype(F32)
        l = [jnp.where(ok & has_left, v[0:1], 0.0), jnp.where(ok, v[1:3], 0.0)]
        g = [jnp.where(ok, v[3:5], 0.0), jnp.where(ok & has_right, v[5:6], 0.0)]
        e = r + 2
        put(z, r, 0, jnp.concatenate(l + [in2[r, 0:2].astype(F32)], 0), jnp.concatenate(
            [from_left[e, 3:4].astype(F32), ht[e, 0:4].astype(F32)], 0), 2)
        put(z, r, 5, jnp.concatenate([in2[r, 2:4].astype(F32)] + g, 0), jnp.concatenate(
            [ht[e, 4:8].astype(F32), from_right[e, 3:4].astype(F32)], 0), 2)
        return carry

    lax.fori_loop(0, 19, two, 0)
    for copy in copies[6:9]:
        copy.wait()
    last = conv(z, 17, groups, held[2 * LAYER_K:3 * LAYER_K], bias[2:3])
    hid[:, 0:3] = (last[:, 0:3] + lt[3:20, 0:3].astype(F32)).astype(BF).astype(F32)
    hid[:, 3:5] = in3[...].astype(F32)
    hid[:, 5:8] = (last[:, 3:6] + lt[3:20, 5:8].astype(F32)).astype(BF).astype(F32)

    wide = hid[...].reshape(HALF * COLS * T, C)
    mean = jnp.mean(wide * wide, -1, keepdims=True)
    normed = (wide * lax.rsqrt(mean + 1e-6)).astype(BF)
    for w, dst in ((wq, qs), (wk, ks), (wv, vs)):
        v = jnp.dot(normed, w[...], preferred_element_type=F32).astype(BF).astype(F32)
        dst[...] = v.reshape(HALF, COLS, T, C)
    for copy in more:
        copy.wait()
    ckw[...] = ck[...].astype(F32)
    cvw[...] = cv[...].astype(F32)
    block = (lax.broadcasted_iota(jnp.int32, (C, C), 0) // HD
             == lax.broadcasted_iota(jnp.int32, (C, C), 1) // HD)
    ones = jnp.where(block, 1.0, 0.0).astype(BF)
    t = lax.broadcasted_iota(jnp.int32, (COLS, T, C), 1)
    scale = HD ** -0.5

    def attend(r, carry):
        q = qs[r] * scale
        k = ks[r]
        v = vs[r]
        products = []
        for f in range(2):
            key = jnp.concatenate(
                [jnp.broadcast_to(ckw[f, r, c:c + 1], (T, C))[None] for c in range(COLS)], 0)
            products.append(q * key)
        for d in range(T):
            products.append(q * (k if d == 0 else pltpu.roll(k, d, 1)))
        flat = jnp.concatenate([p.reshape(COLS * T, C).astype(BF) for p in products], 0)
        sums = jnp.dot(flat, ones, preferred_element_type=F32).reshape(10, COLS, T, C)
        scores = [sums[0], sums[1], sums[2]]
        for d in range(1, T):
            seen = t >= d
            if d == T - 1:
                seen = seen | (t % 2 == 0)
            scores.append(jnp.where(seen, sums[2 + d], -1e30))
        peak = functools.reduce(jnp.maximum, scores)
        weights_ = [jnp.exp(s - peak) for s in scores]
        norm = functools.reduce(jnp.add, weights_)
        acc = weights_[2] * v
        for f in range(2):
            val = jnp.concatenate(
                [jnp.broadcast_to(cvw[f, r, c:c + 1], (T, C))[None] for c in range(COLS)], 0)
            acc = acc + weights_[f] * val
        for d in range(1, T):
            acc = acc + weights_[2 + d] * pltpu.roll(v, d, 1)
        mix[r] = acc / norm
        return carry

    lax.fori_loop(0, HALF, attend, 0)
    mixed = mix[...].reshape(HALF * COLS * T, C).astype(BF)
    done = wide + jnp.dot(mixed, wo[...], preferred_element_type=F32)
    enc[0] = done[:, :128]
    enc[1] = done[:, 128:]

    def turn(r, carry):
        for dst, base in ((mine, 4 * half), (theirs, 4 - 4 * half)):
            for f in range(4):
                v = jnp.concatenate(
                    [enc[lane, pl.ds(r * COLS * T + base + f, COLS, stride=T)]
                     for lane in (0, 1)], 1)
                dst[f, r] = v.astype(BF)
        return carry

    lax.fori_loop(0, HALF, turn, 0)


def local(latent, conv_cache, conv_weight, conv_bias, w_query, w_key, w_value, w_out,
          cache_key, cache_value):
    params = functools.partial(pltpu.CompilerParams)
    cache = conv_cache.reshape(6, ROWS, COLS, C)
    weights = conv_weight.reshape(3 * LAYER_K, C)
    n_row, n_col = lax.axis_size("row"), lax.axis_size("col")

    def device(tm, row):
        return tm * n_row + row

    msg_a, msg_b = pl.pallas_call(
        pack_rows,
        out_shape=(shape(10, 3, COLS, C), shape(4, 3, COLS, C)),
        in_specs=[ANY, ANY],
        out_specs=(ANY, ANY),
        scratch_shapes=[pltpu.SemaphoreType.DMA((3,))],
        name="pack_rows",
    )(latent, cache)
    other = lax.ppermute(latent, "tm", [(0, 1), (1, 0)])
    pairs_a = [(device(0, r), device(0, r + 1)) for r in range(n_row - 1)]
    pairs_a += [(device(1, r + 1), device(1, r)) for r in range(n_row - 1)]
    pairs_b = [(device(1, r), device(0, r + 1)) for r in range(n_row - 1)]
    pairs_b += [(device(0, r + 1), device(1, r)) for r in range(n_row - 1)]
    halo_a = lax.ppermute(msg_a, ("tm", "row"), pairs_a)
    halo_b = lax.ppermute(msg_b, ("tm", "row"), pairs_b)

    tiles = shape(EXT, COLS, T, C)
    side = shape(EXT, 5, T, C)
    lt, ht, left, right = pl.pallas_call(
        assemble,
        out_shape=(tiles, tiles, side, side),
        in_specs=[ANY] * 5,
        out_specs=(VM,) * 4,
        scratch_shapes=[
            pltpu.VMEM((14, EXT, COLS, C), BF),
            pltpu.VMEM((4, 16 * COLS, 128), F32),
            pltpu.SemaphoreType.DMA((6,)),
        ],
        compiler_params=params(vmem_limit_bytes=16 << 20),
        name="assemble",
    )(latent, other, cache, halo_a, halo_b)
    from_right = lax.ppermute(left, "col", [(i + 1, i) for i in range(n_col - 1)])
    from_left = lax.ppermute(right, "col", [(i, i + 1) for i in range(n_col - 1)])

    in1, in2, in3 = pl.pallas_call(
        interior,
        out_shape=(shape(21, 4, T, C), shape(19, 4, T, C), shape(17, 2, T, C)),
        in_specs=[VM, VM, ANY, VM],
        out_specs=(VM,) * 3,
        scratch_shapes=[
            pltpu.VMEM((3, 23, 8, T, C), F32),
            pltpu.VMEM((3, 21, 6, T, C), F32),
            pltpu.VMEM((3, 19, 4, T, C), F32),
            pltpu.VMEM((21, 6, T, C), F32),
            pltpu.VMEM((3 * LAYER_K, C), BF),
            pltpu.SemaphoreType.DMA((9,)),
        ],
        cost_estimate=pl.CostEstimate(
            flops=2 * 1888 * LAYER_K * C, bytes_accessed=14 << 20, transcendentals=0),
        compiler_params=params(vmem_limit_bytes=48 << 20),
        name="interior",
    )(lt, ht, weights, conv_bias)

    pixels = HALF * COLS * T
    mine, theirs = pl.pallas_call(
        exterior,
        out_shape=(shape(4, HALF, COLS, C), shape(4, HALF, COLS, C)),
        in_specs=[VM] * 7 + [ANY] + [VM] * 5 + [ANY] * 2,
        out_specs=(VM, VM),
        scratch_shapes=[
            pltpu.VMEM((3, 23, 10, T, C), F32),
            pltpu.VMEM((3, 21, 10, T, C), F32),
            pltpu.VMEM((3, 19, 10, T, C), F32),
            pltpu.VMEM((21, 6, T, C), F32),
            pltpu.VMEM((3 * LAYER_K, C), BF),
            pltpu.VMEM((HALF, COLS, T, C), F32),
            pltpu.VMEM((HALF, COLS, T, C), F32),
            pltpu.VMEM((HALF, COLS, T, C), F32),
            pltpu.VMEM((HALF, COLS, T, C), F32),
            pltpu.VMEM((HALF, COLS, T, C), F32),
            pltpu.VMEM((2, HALF, COLS, C), BF),
            pltpu.VMEM((2, HALF, COLS, C), BF),
            pltpu.VMEM((2, HALF, COLS, C), F32),
            pltpu.VMEM((2, HALF, COLS, C), F32),
            pltpu.VMEM((2, pixels, 128), F32),
            pltpu.SemaphoreType.DMA((11,)),
        ],
        cost_estimate=pl.CostEstimate(
            flops=2 * 3000 * LAYER_K * C, bytes_accessed=18 << 20, transcendentals=0),
        compiler_params=params(vmem_limit_bytes=56 << 20),
        name="exterior",
    )(lt, ht, from_left, from_right, in1, in2, in3, weights, conv_bias, w_query, w_key, w_value,
      w_out, cache_key, cache_value)
    got = lax.ppermute(theirs, "tm", [(0, 1), (1, 0)])
    top = lax.axis_index("tm") == 0
    return jnp.concatenate([jnp.where(top, mine, got), jnp.where(top, got, mine)], 1)


def solution(mesh):
    return jax.shard_map(
        local,
        mesh=mesh,
        in_specs=(
            P("tm", "row", "col", None),
            P(None, None, "row", "col", None),
            P(),
            P(),
            P(),
            P(),
            P(),
            P(),
            P(None, "row", "col", None),
            P(None, "row", "col", None),
        ),
        out_specs=P("tm", "row", "col", None),
        check_vma=False,
    )
```

profile of v0, /device:TPU:131, one launch (start us, length us, event | category | flops | bytes accessed | tf_op | source)
XLA Modules:
  0.0 85.4 jit_solution(10290329514233071215)
XLA Ops:
  0.0 0.7 collective-permute-start
  0.7 6.3 %pack_rows.1 = (bf16[10,3,8,256]{3,2,1,0:T(8,128)(2,1)}, bf16[4,3,8,256]{3,2,1,0:T(8,128)(2,1)}) custom-call(bf16[4,34,8,256]{3,2,1,0:T(8,128)(2,1)} %own.1, bf16[6,34,8,256]{3,2,1,0:T(8,128)(2,1)} %bitcast.2), custom_call_target="tpu_custom_call" | custom-call | tf_op jit(solution)/shard_map/pack_rows/pallas_call | solution.py:349
  7.0 2.2 %collective-permute-start.1 = (bf16[10,3,8,256]{3,2,1,0:T(8,128)(2,1)}, bf16[10,3,8,256]{3,2,1,0:T(8,128)(2,1)S(1)}, u32[]{:S(2)}, u32[]{:S(2)}) collective-permute-start(bf16[10,3,8,256]{3,2,1,0:T(8,128)(2,1)} %get-tuple-element.16), channel_id=1, source_target_pairs={{0,32},{32,64},{64,96},{160,128},{192,160},{224,192},{1,33},{33,65... | collective-permute-start | bytes 368648 | tf_op jit(solution)/shard_map/ppermute | solution.py:362
  9.2 4.0 %collective-permute-start.2 = (bf16[4,3,8,256]{3,2,1,0:T(8,128)(2,1)}, bf16[4,3,8,256]{3,2,1,0:T(8,128)(2,1)S(1)}, u32[]{:S(2)}, u32[]{:S(2)}) collective-permute-start(bf16[4,3,8,256]{3,2,1,0:T(8,128)(2,1)} %get-tuple-element.17), channel_id=1, source_target_pairs={{128,32},{160,64},{192,96},{32,128},{64,160},{96,192},{129,33},{16... | collective-permute-start | bytes 147464 | tf_op jit(solution)/shard_map/ppermute | solution.py:363
  13.1 2.3 %collective-permute-done.2.halo_b = bf16[4,3,8,256]{3,2,1,0:T(8,128)(2,1)S(1)} collective-permute-done((bf16[4,3,8,256]{3,2,1,0:T(8,128)(2,1)}, bf16[4,3,8,256]{3,2,1,0:T(8,128)(2,1)S(1)}, u32[]{:S(2)}, u32[]{:S(2)}) %collective-permute-start.2) | collective-permute-done | bytes 49184 | tf_op jit(solution)/shard_map/ppermute | solution.py:363
  15.4 0.0 collective-permute-done.1.halo_a
  15.4 0.0 collective-permute-done.other
  15.4 0.0 copy-start
  15.4 1.1 %copy-done = bf16[3,2,34,8,256]{4,3,2,1,0:T(8,128)(2,1)S(1)} copy-done((bf16[3,2,34,8,256]{4,3,2,1,0:T(8,128)(2,1)S(1)}, bf16[3,2,34,8,256]{4,3,2,1,0:T(8,128)(2,1)}, u32[]{:S(2)}) %copy-start) | copy-done | bytes 835608
  16.6 0.0 copy-start.1
  16.6 1.1 %copy-done.1 = bf16[4,34,8,256]{3,2,1,0:T(8,128)(2,1)S(1)} copy-done((bf16[4,34,8,256]{3,2,1,0:T(8,128)(2,1)S(1)}, bf16[4,34,8,256]{3,2,1,0:T(8,128)(2,1)}, u32[]{:S(2)}) %copy-start.1) | copy-done | bytes 557080
  17.6 1.0 %assemble.1 = (bf16[23,8,8,256]{3,2,1,0:T(8,128)(2,1)S(1)}, bf16[23,8,8,256]{3,2,1,0:T(8,128)(2,1)S(1)}, bf16[23,5,8,256]{3,2,1,0:T(8,128)(2,1)S(1)}, bf16[23,5,8,256]{3,2,1,0:T(8,128)(2,1)S(1)}) custom-call(bf16[4,34,8,256]{3,2,1,0:T(8,128)(2,1)S(1)} %copy-done.1, bf16[4,34,8,256]{3,2,1,0:T(8,128)(2,1)S(1)} %collective-permute-done.other, ...), custom_call_target="tpu_custom_call" | custom-call | tf_op jit(solution)/shard_map/assemble/pallas_call | solution.py:367
  18.6 0.0 copy-start.2
  18.6 0.0 copy-start.3
  18.6 3.2 %collective-permute-start.3 = (bf16[23,5,8,256]{3,2,1,0:T(8,128)(2,1)S(1)}, bf16[23,5,8,256]{3,2,1,0:T(8,128)(2,1)S(1)}, u32[]{:S(2)}, u32[]{:S(2)}) collective-permute-start(bf16[23,5,8,256]{3,2,1,0:T(8,128)(2,1)S(1)} %get-tuple-element.20), channel_id=1, source_target_pairs={{0,1},{1,2},{2,3},{3,4},{4,5},{5,6},{6,7},{7,8},{8,9},{9,10},{10,1... | collective-permute-start | bytes 1413128 | tf_op jit(solution)/shard_map/ppermute | solution.py:381
  21.8 5.4 %collective-permute-start.4 = (bf16[23,5,8,256]{3,2,1,0:T(8,128)(2,1)S(1)}, bf16[23,5,8,256]{3,2,1,0:T(8,128)(2,1)S(1)}, u32[]{:S(2)}, u32[]{:S(2)}) collective-permute-start(bf16[23,5,8,256]{3,2,1,0:T(8,128)(2,1)S(1)} %get-tuple-element.21), channel_id=1, source_target_pairs={{1,0},{2,1},{3,2},{4,3},{5,4},{6,5},{7,6},{8,7},{9,8},{10,9},{11,1... | collective-permute-start | bytes 1413128 | tf_op jit(solution)/shard_map/ppermute | solution.py:380
  27.2 0.0 copy-start.4
  27.2 0.7 copy-done.4
  27.9 16.7 %interior.1 = (bf16[21,4,8,256]{3,2,1,0:T(8,128)(2,1)S(1)}, bf16[19,4,8,256]{3,2,1,0:T(8,128)(2,1)S(1)}, bf16[17,2,8,256]{3,2,1,0:T(8,128)(2,1)S(1)}) custom-call(bf16[23,8,8,256]{3,2,1,0:T(8,128)(2,1)S(1)} %get-tuple-element.18.lt, bf16[23,8,8,256]{3,2,1,0:T(8,128)(2,1)S(1)} %get-tuple-element.19.ht, bf16[20736,256]{1,0:T(8,128)(2,1)} %bitcast.4, ...), custom_call_target="tpu_custom_call" | custom-call | flops 6681526272 | bytes 14680064 | tf_op jit(solution)/shard_map/interior/pallas_call | solution.py:383
  44.7 0.0 copy-done.2
  44.7 0.0 copy-done.3
  44.7 0.0 copy-start.5
  44.7 0.7 copy-done.5
  45.4 0.0 copy-start.6
  45.4 0.7 copy-done.6
  46.1 0.0 copy-start.7
  46.1 0.6 copy-done.7
  46.8 0.0 collective-permute-done.3.from_left
  46.8 0.0 copy-start.8
  46.8 0.0 collective-permute-done.4.from_right
  46.8 0.0 copy-start.9
  46.8 0.8 copy-done.8
  47.6 0.2 copy-done.9
  47.7 33.2 %exterior.1 = (bf16[4,17,8,256]{3,2,1,0:T(8,128)(2,1)}, bf16[4,17,8,256]{3,2,1,0:T(8,128)(2,1)}) custom-call(bf16[23,8,8,256]{3,2,1,0:T(8,128)(2,1)} %copy-done.2, bf16[23,8,8,256]{3,2,1,0:T(8,128)(2,1)} %copy-done.3, bf16[23,5,8,256]{3,2,1,0:T(8,128)(2,1)} %copy-done.8, bf16[23,5,8,256]{3,2,1,0:T(8,128)(2,1)} %copy-done.9, ...), custom_call_target="tpu_custom_call" | custom-call | flops 10616832000 | bytes 18874368 | tf_op jit(solution)/shard_map/exterior/pallas_call | solution.py:403
  80.9 1.3 %collective-permute-start.5 = (bf16[4,17,8,256]{3,2,1,0:T(8,128)(2,1)}, bf16[4,17,8,256]{3,2,1,0:T(8,128)(2,1)S(1)}, u32[]{:S(2)}, u32[]{:S(2)}) collective-permute-start(bf16[4,17,8,256]{3,2,1,0:T(8,128)(2,1)} %get-tuple-element.26), channel_id=1, source_target_pairs={{0,128},{128,0},{1,129},{129,1},{2,130},{130,2},{3,131},{131,3},{4... | collective-permute-start | bytes 835592 | tf_op jit(solution)/shard_map/ppermute | solution.py:432
  82.2 1.4 %collective-permute-done.5 = bf16[4,17,8,256]{3,2,1,0:T(8,128)(2,1)S(1)} collective-permute-done((bf16[4,17,8,256]{3,2,1,0:T(8,128)(2,1)}, bf16[4,17,8,256]{3,2,1,0:T(8,128)(2,1)S(1)}, u32[]{:S(2)}, u32[]{:S(2)}) %collective-permute-start.5) | collective-permute-done | bytes 278560 | tf_op jit(solution)/shard_map/ppermute | solution.py:432
  83.6 1.0 %broadcast_select_fusion.1 = (bf16[4,17,8,256]{3,2,1,0:T(8,128)(2,1)S(1)}, bf16[4,17,8,256]{3,2,1,0:T(8,128)(2,1)S(1)}) fusion(bf16[4,17,8,256]{3,2,1,0:T(8,128)(2,1)} %get-tuple-element.25, bf16[4,17,8,256]{3,2,1,0:T(8,128)(2,1)S(1)} %collective-permute-done.5, pred[]{:T(512)S(6)} %eq.3), kind=kLoop, calls=%fused_computation.2 | loop fusion | flops 278528 | bytes 1114113 | tf_op jit(solution)/shard_map/jit(_where)/select_n | solution.py:434
  84.6 0.9 %pad_maximum_fusion = bf16[4,34,8,256]{3,2,1,0:T(8,128)(2,1)} fusion(bf16[4,17,8,256]{3,2,1,0:T(8,128)(2,1)S(1)} %get-tuple-element.28, bf16[4,17,8,256]{3,2,1,0:T(8,128)(2,1)S(1)} %get-tuple-element.27), kind=kLoop, calls=%fused_computation | loop fusion | flops 278528 | bytes 1114112 | tf_op jit(solution)/shard_map/concatenate | solution.py:434
Async XLA Ops:
  0.0 15.4 %collective-permute-start = (bf16[4,34,8,256]{3,2,1,0:T(8,128)(2,1)}, bf16[4,34,8,256]{3,2,1,0:T(8,128)(2,1)S(1)}, u32[]{:S(2)}, u32[]{:S(2)}) collective-permute-start(bf16[4,34,8,256]{3,2,1,0:T(8,128)(2,1)} %own.1), channel_id=1, source_target_pairs={{0,128},{128,0},{1,129},{129,1},{2,130},{130,2},{3,131},{131,3},{4... | collective-permute-start | bytes 1671176 | tf_op jit(solution)/shard_map/ppermute | solution.py:357
  7.0 8.4 %collective-permute-start.1 = (bf16[10,3,8,256]{3,2,1,0:T(8,128)(2,1)}, bf16[10,3,8,256]{3,2,1,0:T(8,128)(2,1)S(1)}, u32[]{:S(2)}, u32[]{:S(2)}) collective-permute-start(bf16[10,3,8,256]{3,2,1,0:T(8,128)(2,1)} %get-tuple-element.16), channel_id=1, source_target_pairs={{0,32},{32,64},{64,96},{160,128},{192,160},{224,192},{1,33},{33,65... | collective-permute-start | bytes 368648 | tf_op jit(solution)/shard_map/ppermute | solution.py:362
  9.2 6.2 %collective-permute-start.2 = (bf16[4,3,8,256]{3,2,1,0:T(8,128)(2,1)}, bf16[4,3,8,256]{3,2,1,0:T(8,128)(2,1)S(1)}, u32[]{:S(2)}, u32[]{:S(2)}) collective-permute-start(bf16[4,3,8,256]{3,2,1,0:T(8,128)(2,1)} %get-tuple-element.17), channel_id=1, source_target_pairs={{128,32},{160,64},{192,96},{32,128},{64,160},{96,192},{129,33},{16... | collective-permute-start | bytes 147464 | tf_op jit(solution)/shard_map/ppermute | solution.py:363
  15.4 1.2 %copy-start = (bf16[3,2,34,8,256]{4,3,2,1,0:T(8,128)(2,1)S(1)}, bf16[3,2,34,8,256]{4,3,2,1,0:T(8,128)(2,1)}, u32[]{:S(2)}) copy-start(bf16[3,2,34,8,256]{4,3,2,1,0:T(8,128)(2,1)} %param.11) | copy-start | bytes 2506756
  16.6 1.1 %copy-start.1 = (bf16[4,34,8,256]{3,2,1,0:T(8,128)(2,1)S(1)}, bf16[4,34,8,256]{3,2,1,0:T(8,128)(2,1)}, u32[]{:S(2)}) copy-start(bf16[4,34,8,256]{3,2,1,0:T(8,128)(2,1)} %own.1) | copy-start | bytes 1671172
  18.6 26.1 %copy-start.2 = (bf16[23,8,8,256]{3,2,1,0:T(8,128)(2,1)}, bf16[23,8,8,256]{3,2,1,0:T(8,128)(2,1)S(1)}, u32[]{:S(2)}) copy-start(bf16[23,8,8,256]{3,2,1,0:T(8,128)(2,1)S(1)} %get-tuple-element.18.lt) | copy-start | bytes 2260996
  18.6 26.1 %copy-start.3 = (bf16[23,8,8,256]{3,2,1,0:T(8,128)(2,1)}, bf16[23,8,8,256]{3,2,1,0:T(8,128)(2,1)S(1)}, u32[]{:S(2)}) copy-start(bf16[23,8,8,256]{3,2,1,0:T(8,128)(2,1)S(1)} %get-tuple-element.19.ht) | copy-start | bytes 2260996
  18.6 28.2 %collective-permute-start.3 = (bf16[23,5,8,256]{3,2,1,0:T(8,128)(2,1)S(1)}, bf16[23,5,8,256]{3,2,1,0:T(8,128)(2,1)S(1)}, u32[]{:S(2)}, u32[]{:S(2)}) collective-permute-start(bf16[23,5,8,256]{3,2,1,0:T(8,128)(2,1)S(1)} %get-tuple-element.20), channel_id=1, source_target_pairs={{0,1},{1,2},{2,3},{3,4},{4,5},{5,6},{6,7},{7,8},{8,9},{9,10},{10,1... | collective-permute-start | bytes 1413128 | tf_op jit(solution)/shard_map/ppermute | solution.py:381
  21.8 25.0 %collective-permute-start.4 = (bf16[23,5,8,256]{3,2,1,0:T(8,128)(2,1)S(1)}, bf16[23,5,8,256]{3,2,1,0:T(8,128)(2,1)S(1)}, u32[]{:S(2)}, u32[]{:S(2)}) collective-permute-start(bf16[23,5,8,256]{3,2,1,0:T(8,128)(2,1)S(1)} %get-tuple-element.21), channel_id=1, source_target_pairs={{1,0},{2,1},{3,2},{4,3},{5,4},{6,5},{7,6},{8,7},{9,8},{10,9},{11,1... | collective-permute-start | bytes 1413128 | tf_op jit(solution)/shard_map/ppermute | solution.py:380
  27.2 0.7 copy-start.4
  44.7 0.7 copy-start.5
  45.4 0.7 copy-start.6
  46.1 0.6 copy-start.7
  46.8 0.8 copy-start.8
  46.8 0.9 %copy-start.9 = (bf16[23,5,8,256]{3,2,1,0:T(8,128)(2,1)}, bf16[23,5,8,256]{3,2,1,0:T(8,128)(2,1)S(1)}, u32[]{:S(2)}) copy-start(bf16[23,5,8,256]{3,2,1,0:T(8,128)(2,1)S(1)} %collective-permute-done.4.from_right) | copy-start | bytes 1413124
  80.9 2.7 %collective-permute-start.5 = (bf16[4,17,8,256]{3,2,1,0:T(8,128)(2,1)}, bf16[4,17,8,256]{3,2,1,0:T(8,128)(2,1)S(1)}, u32[]{:S(2)}, u32[]{:S(2)}) collective-permute-start(bf16[4,17,8,256]{3,2,1,0:T(8,128)(2,1)} %get-tuple-element.26), channel_id=1, source_target_pairs={{0,128},{128,0},{1,129},{129,1},{2,130},{130,2},{3,131},{131,3},{4... | collective-permute-start | bytes 835592 | tf_op jit(solution)/shard_map/ppermute | solution.py:432
where the time goes:
time: 85.8 us; the launch traced here: 85.4 us
  Pallas kernels  57.2 us (67%)
  starting transfers between devices  16.7 us (19%)
  local copies, waits for them, and re-layouts  5.92 us (7%)
  waiting for transfers between devices  3.67 us (4%)
  other arithmetic  1.85 us (2%)
    pallas_call x1, Pallas kernels, local(): pl.pallas_call(exterior, out_shape=(shape(4, HALF, COLS, C), shape(4, HAL...  33.2 us
    pallas_call x1, Pallas kernels, local(): pl.pallas_call(interior, out_shape=(shape(21, 4, T, C), shape(19, 4, T, C...  16.7 us
    pallas_call x1, Pallas kernels, local(): pl.pallas_call(pack_rows, out_shape=(shape(10, 3, COLS, C), shape(4, 3, C...  6.34 us
    unnamed x20, local copies, waits for them, and re-layouts  5.92 us
    ppermute x1, starting transfers between devices, local(): lax.ppermute(left, 'col', [(i + 1, i) for i in range(n_col - 1)])  5.4 us
    ppermute x1, starting transfers between devices, local(): halo_b = lax.ppermute(msg_b, ('tm', 'row'), pairs_b)  3.95 us
    ppermute x1, starting transfers between devices, local(): lax.ppermute(right, 'col', [(i, i + 1) for i in range(n_col - 1)])  3.2 us
    ppermute x1, waiting for transfers between devices, local(): halo_b = lax.ppermute(msg_b, ('tm', 'row'), pairs_b)  2.26 us
  transfers between devices with their start and end apart: 6, of which 2 were waited for; matrix products, arithmetic and copies ran while one was open for 0% of the time, Pallas kernels for 27%

commit v1 on v0

v1 whole, which is shorter than its diff:
```python
import functools

import jax
import jax.numpy as jnp
from jax import lax
from jax.experimental import pallas as pl
from jax.experimental.pallas import tpu as pltpu
from jax.sharding import PartitionSpec as P

HEADS = 8
HD = 32
C = 256
T = 8
FRAMES = 4
ROWS = 34
HALF = 17
COLS = 8
EXT = HALF + 6
BF = jnp.bfloat16
F32 = jnp.float32
TAPS = [(a, b, c) for a in range(3) for b in range(3) for c in range(3)]
LAYER_K = 27 * C

ANY = pl.BlockSpec(memory_space=pl.ANY)
HB = pl.BlockSpec(memory_space=pltpu.HBM)
VM = pl.BlockSpec(memory_space=pltpu.VMEM)


def shape(*dims, dtype=BF):
    return jax.ShapeDtypeStruct(dims, dtype)


def run_copies(copies):
    for copy in copies:
        copy.start()
    for copy in copies:
        copy.wait()


def pack_rows(latent, cache, out_a, out_b, own, old, sems):
    half = lax.axis_index("tm")
    row_a, row_b, start = 31 * (1 - half), 31 * half, 14 * half
    run_copies([
        pltpu.make_async_copy(latent.at[:, pl.ds(row_a, 3)], out_a.at[0:4], sems.at[0]),
        pltpu.make_async_copy(cache.at[:, pl.ds(row_a, 3)], out_a.at[4:10], sems.at[1]),
        pltpu.make_async_copy(latent.at[:, pl.ds(row_b, 3)], out_b, sems.at[2]),
        pltpu.make_async_copy(latent.at[:, pl.ds(start, 20)], own, sems.at[3]),
        pltpu.make_async_copy(cache.at[:, pl.ds(start, 20)], old, sems.at[4]),
    ])


def load_weights(weights, bias, held, held_bias, sems):
    run_copies([
        pltpu.make_async_copy(weights, held, sems.at[0]),
        pltpu.make_async_copy(bias, held_bias, sems.at[1]),
    ])


def assemble(own, other, cache, halo_a, halo_b, held, lt, ht, left, right, kept, stage, wide, sems):
    half = lax.axis_index("tm")
    first, second = 4 * half, 4 - 4 * half
    start, at, edge = 14 * half, 3 - 3 * half, 20 * half
    run_copies([
        pltpu.make_async_copy(
            own, stage.at[pl.ds(first, 4), pl.ds(at, 20)], sems.at[0]),
        pltpu.make_async_copy(
            other.at[:, pl.ds(start, 20)], stage.at[pl.ds(second, 4), pl.ds(at, 20)], sems.at[1]),
        pltpu.make_async_copy(
            cache, stage.at[8:14, pl.ds(at, 20)], sems.at[2]),
        pltpu.make_async_copy(
            halo_a.at[0:4], stage.at[pl.ds(first, 4), pl.ds(edge, 3)], sems.at[3]),
        pltpu.make_async_copy(halo_a.at[4:10], stage.at[8:14, pl.ds(edge, 3)], sems.at[4]),
        pltpu.make_async_copy(
            halo_b, stage.at[pl.ds(second, 4), pl.ds(edge, 3)], sems.at[5]),
    ])
    sub = lax.broadcasted_iota(jnp.int32, (T, C), 0)
    for slot in range(4):
        wide[slot, 14 * COLS:16 * COLS] = jnp.zeros((2 * COLS, 128), F32)

    def row(e, slot):
        for frame in range(14):
            v = stage[frame, e].astype(F32)
            wide[2 * slot, frame * COLS:(frame + 1) * COLS] = v[:, :128]
            wide[2 * slot + 1, frame * COLS:(frame + 1) * COLS] = v[:, 128:]
        past = []
        for col in range(COLS):
            lat = jnp.concatenate(
                [wide[2 * slot + lane, pl.ds(col, T, stride=COLS)] for lane in (0, 1)], 1)
            old = jnp.concatenate(
                [wide[2 * slot + lane, pl.ds(T * COLS + col, T, stride=COLS)]
                 for lane in (0, 1)], 1)
            lt[e, col] = lat.astype(BF)
            ht[e, col] = old.astype(BF)
            past.append(old)
            if col < 3:
                left[e, col] = lat.astype(BF)
            if col >= 5:
                right[e, col - 5] = lat.astype(BF)
        left[e, 3] = jnp.where(sub < 6, past[0], pltpu.roll(past[2], 6, 0)).astype(BF)
        left[e, 4] = past[1].astype(BF)
        right[e, 3] = jnp.where(sub < 6, past[7], pltpu.roll(past[5], 6, 0)).astype(BF)
        right[e, 4] = past[6].astype(BF)

    def pair(i, carry):
        row(2 * i, 0)
        row(2 * i + 1, 1)
        return carry

    lax.fori_loop(0, EXT // 2, pair, 0)
    row(EXT - 1, 0)


def put(dst, r, at, now, past, layer):
    n = now.shape[0]
    sub = lax.broadcasted_iota(jnp.int32, (n, T, C), 1)

    def roll(v, k):
        k %= T
        return v if k == 0 else pltpu.roll(v, k, 1)

    dst[2, r, at:at + n] = now
    dst[1, r, at:at + n] = jnp.where(sub < 1, roll(past, -2 * layer - 1), roll(now, 1))
    dst[0, r, at:at + n] = jnp.where(sub < 2, roll(past, -2 * layer), roll(now, 2))


def conv(src, rows, groups, held, layer, bias, dst):
    count = sum(n for _, n in groups)
    step = (rows + 1) // 2

    def body(i, carry):
        r = i * (rows - step)
        total = None
        for a in range(3):
            for b in range(3):
                parts = []
                for c in range(3):
                    cols = [src[a, pl.ds(r + b, step), first + c:first + c + n]
                            for first, n in groups]
                    block = cols[0] if len(cols) == 1 else jnp.concatenate(cols, 1)
                    parts.append(block.reshape(step * count * T, C).astype(BF))
                k = layer * LAYER_K + (a * 3 + b) * 3 * C
                part = jnp.dot(
                    jnp.concatenate(parts, 1), held[k:k + 3 * C], preferred_element_type=F32)
                total = part if total is None else total + part
        dst[pl.ds(r, step), 0:count] = (total + bias).reshape(step, count, T, C)
        return carry

    lax.fori_loop(0, 2, body, 0)


def silu(v):
    return v / (1.0 + jnp.exp(-v))


def row_limits(border):
    half, place = lax.axis_index("tm"), lax.axis_index("row")
    low = jnp.where((half == 0) & (place == 0), border, 0)
    high = jnp.where(
        (half == 1) & (place == lax.axis_size("row") - 1), HALF + border, HALF + 2 * border)
    return low, high


def attend_all(hidden, cols, rows, wq, wk, wv, wo, keys, values, qs, ks, vs, mix):
    n = len(cols)
    mean = jnp.mean(hidden * hidden, -1, keepdims=True)
    normed = (hidden * lax.rsqrt(mean + 1e-6)).astype(BF)
    for w, dst in ((wq, qs), (wk, ks), (wv, vs)):
        v = jnp.dot(normed, w[...], preferred_element_type=F32).astype(BF).astype(F32)
        dst[0:HALF] = v.reshape(HALF, n, T, C)
        dst[HALF:] = jnp.zeros((1, n, T, C), F32)
    block = (lax.broadcasted_iota(jnp.int32, (C, C), 0) // HD
             == lax.broadcasted_iota(jnp.int32, (C, C), 1) // HD)
    ones = jnp.where(block, 1.0, 0.0).astype(BF)
    m = rows * n
    t = lax.broadcasted_iota(jnp.int32, (m, T, C), 1)

    def attend(i, carry):
        r = rows * i
        q = qs[pl.ds(r, rows)].reshape(m, T, C) * HD ** -0.5
        k = ks[pl.ds(r, rows)].reshape(m, T, C)
        v = vs[pl.ds(r, rows)].reshape(m, T, C)

        def spread(ref, f):
            return jnp.concatenate(
                [jnp.broadcast_to(ref[f, r + j, c:c + 1], (T, C))[None]
                 for j in range(rows) for c in cols], 0)

        products = [q * spread(keys, f) for f in range(2)]
        for d in range(T):
            products.append(q * (k if d == 0 else pltpu.roll(k, d, 1)))
        flat = jnp.concatenate([p.reshape(m * T, C).astype(BF) for p in products], 0)
        sums = jnp.dot(flat, ones, preferred_element_type=F32).reshape(10, m, T, C)
        scores = [sums[0], sums[1], sums[2]]
        for d in range(1, T):
            seen = t >= d
            if d == T - 1:
                seen = seen | (t % 2 == 0)
            scores.append(jnp.where(seen, sums[2 + d], -1e30))
        peak = functools.reduce(jnp.maximum, scores)
        weights = [jnp.exp(s - peak) for s in scores]
        norm = functools.reduce(jnp.add, weights)
        acc = weights[2] * v
        for f in range(2):
            acc = acc + weights[f] * spread(values, f)
        for d in range(1, T):
            acc = acc + weights[2 + d] * pltpu.roll(v, d, 1)
        mix[pl.ds(r, rows)] = (acc / norm).reshape(rows, n, T, C)
        return carry

    lax.fori_loop(0, (HALF + 1) // rows, attend, 0)
    mixed = mix[0:HALF].reshape(HALF * n * T, C).astype(BF)
    return hidden + jnp.dot(mixed, wo[...], preferred_element_type=F32)


def interior(lt, ht, held, bias, wq, wk, wv, wo, key_cache, value_cache, out, kept, x, y, z,
             keys, values, res, qs, ks, vs, mix, ck, cv, sems):
    del kept
    half = lax.axis_index("tm")
    copies = [
        pltpu.make_async_copy(key_cache.at[:, pl.ds(HALF * half, HALF)], ck, sems.at[0]),
        pltpu.make_async_copy(value_cache.at[:, pl.ds(HALF * half, HALF)], cv, sems.at[1]),
    ]
    for copy in copies:
        copy.start()

    def fill(r, carry):
        put(x, r, 3, lt[r].astype(F32), ht[r].astype(F32), 0)
        return carry

    lax.fori_loop(0, EXT, fill, 0)
    conv(x, 21, [(3, 6)], held, 0, bias[0:1], res)
    low, high = row_limits(2)

    def one(r, carry):
        v = jnp.where((r >= low) & (r < high), silu(res[r]), 0.0).astype(BF)
        put(y, r, 3, v.astype(F32), ht[r + 1, 1:7].astype(F32), 1)
        return carry

    lax.fori_loop(0, 21, one, 0)
    conv(y, 19, [(3, 4)], held, 1, bias[1:2], res)
    low2, high2 = row_limits(1)

    def two(r, carry):
        v = jnp.where((r >= low2) & (r < high2), silu(res[r, 0:4]), 0.0).astype(BF)
        put(z, r, 3, v.astype(F32), ht[r + 2, 2:6].astype(F32), 2)
        return carry

    lax.fori_loop(0, 19, two, 0)
    conv(z, 17, [(3, 2)], held, 2, bias[2:3], res)
    hidden = (res[0:17, 0:2] + lt[3:20, 3:5].astype(F32)).astype(BF).astype(F32)
    for copy in copies:
        copy.wait()
    for src, dst in ((ck, keys), (cv, values)):
        dst[:, 0:HALF] = src[...].astype(F32)
        dst[:, HALF:] = jnp.zeros((2, 1, COLS, C), F32)
    done = attend_all(hidden.reshape(HALF * 2 * T, C), (3, 4), 9, wq, wk, wv, wo, keys, values,
                      qs, ks, vs, mix)
    out[...] = done.reshape(HALF, 2, T, C).astype(BF)


def exterior(lt, ht, from_left, from_right, inner, held, bias, wq, wk, wv, wo, x0, y0, z0,
             keys, values, mine, theirs, x, y, z, res, qs, ks, vs, mix, enc):
    del x0, y0, z0
    half = lax.axis_index("tm")
    place = lax.axis_index("col")
    has_left = place > 0
    has_right = place < lax.axis_size("col") - 1

    def fill(r, carry):
        for side, at in ((from_left, 0), (from_right, 11)):
            t1 = side[r, 3].astype(F32)
            t2 = side[r, 4].astype(F32)
            t3 = pltpu.roll(t1, 2, 0)
            order = (t3, t2, t1) if at == 0 else (t1, t2, t3)
            past = jnp.concatenate([v[None] for v in order], 0)
            put(x, r, at, side[r, 0:3].astype(F32), past, 0)
        return carry

    lax.fori_loop(0, EXT, fill, 0)
    conv(x, 21, [(0, 3), (9, 3)], held, 0, bias[0:1], res)
    low, high = row_limits(2)

    def one(r, carry):
        ok = (r >= low) & (r < high)
        v = silu(res[r]).astype(BF).astype(F32)
        e = r + 1
        put(y, r, 0, jnp.concatenate(
            [jnp.where(ok & has_left, v[0:2], 0.0), jnp.where(ok, v[2:3], 0.0)], 0),
            jnp.concatenate([from_left[e, 4:5].astype(F32), from_left[e, 3:4].astype(F32),
                             ht[e, 0:1].astype(F32)], 0), 1)
        put(y, r, 9, jnp.concatenate(
            [jnp.where(ok, v[3:4], 0.0), jnp.where(ok & has_right, v[4:6], 0.0)], 0),
            jnp.concatenate([ht[e, 7:8].astype(F32), from_right[e, 3:4].astype(F32),
                             from_right[e, 4:5].astype(F32)], 0), 1)
        return carry

    lax.fori_loop(0, 21, one, 0)
    conv(y, 19, [(0, 3), (7, 3)], held, 1, bias[1:2], res)
    low2, high2 = row_limits(1)

    def two(r, carry):
        ok = (r >= low2) & (r < high2)
        v = silu(res[r]).astype(BF).astype(F32)
        e = r + 2
        put(z, r, 0, jnp.concatenate(
            [jnp.where(ok & has_left, v[0:1], 0.0), jnp.where(ok, v[1:3], 0.0)], 0),
            jnp.concatenate([from_left[e, 3:4].astype(F32), ht[e, 0:2].astype(F32)], 0), 2)
        put(z, r, 7, jnp.concatenate(
            [jnp.where(ok, v[3:5], 0.0), jnp.where(ok & has_right, v[5:6], 0.0)], 0),
            jnp.concatenate([ht[e, 6:8].astype(F32), from_right[e, 3:4].astype(F32)], 0), 2)
        return carry

    lax.fori_loop(0, 19, two, 0)
    conv(z, 17, [(0, 3), (5, 3)], held, 2, bias[2:3], res)
    cols = (0, 1, 2, 5, 6, 7)
    own = jnp.concatenate([lt[3:20, 0:3], lt[3:20, 5:8]], 1).astype(F32)
    hidden = (res[0:17] + own).astype(BF).astype(F32)
    done = attend_all(hidden.reshape(HALF * 6 * T, C), cols, 3, wq, wk, wv, wo, keys, values,
                      qs, ks, vs, mix).reshape(HALF, 6, T, C)
    done = jnp.concatenate([done[:, 0:3], inner[...].astype(F32), done[:, 3:6]], 1)
    done = done.reshape(HALF * COLS * T, C)
    enc[0] = done[:, :128]
    enc[1] = done[:, 128:]

    def turn(r, carry):
        for dst, base in ((mine, 4 * half), (theirs, 4 - 4 * half)):
            for f in range(4):
                v = jnp.concatenate(
                    [enc[lane, pl.ds(r * COLS * T + base + f, COLS, stride=T)]
                     for lane in (0, 1)], 1)
                dst[f, r] = v.astype(BF)
        return carry

    lax.fori_loop(0, HALF, turn, 0)


def merge(mine, got, out, sems):
    half = lax.axis_index("tm")
    run_copies([
        pltpu.make_async_copy(mine, out.at[:, pl.ds(HALF * half, HALF)], sems.at[0]),
        pltpu.make_async_copy(got, out.at[:, pl.ds(HALF - HALF * half, HALF)], sems.at[1]),
    ])


def local(latent, conv_cache, conv_weight, conv_bias, w_query, w_key, w_value, w_out,
          cache_key, cache_value):
    params = functools.partial(pltpu.CompilerParams)
    cache = conv_cache.reshape(6, ROWS, COLS, C)
    weights = conv_weight.reshape(3 * LAYER_K, C)
    n_row, n_col = lax.axis_size("row"), lax.axis_size("col")

    def device(tm, row):
        return tm * n_row + row

    msg_a, msg_b, own, old = pl.pallas_call(
        pack_rows,
        out_shape=(shape(10, 3, COLS, C), shape(4, 3, COLS, C), shape(4, 20, COLS, C),
                   shape(6, 20, COLS, C)),
        in_specs=[HB, HB],
        out_specs=(VM,) * 4,
        scratch_shapes=[pltpu.SemaphoreType.DMA((5,))],
        compiler_params=params(vmem_limit_bytes=105 << 19),
        name="pack_rows",
    )(latent, cache)
    other = lax.ppermute(latent, "tm", [(0, 1), (1, 0)])
    pairs_a = [(device(0, r), device(0, r + 1)) for r in range(n_row - 1)]
    pairs_a += [(device(1, r + 1), device(1, r)) for r in range(n_row - 1)]
    pairs_b = [(device(1, r), device(0, r + 1)) for r in range(n_row - 1)]
    pairs_b += [(device(0, r + 1), device(1, r)) for r in range(n_row - 1)]
    halo_a = lax.ppermute(msg_a, ("tm", "row"), pairs_a)
    halo_b = lax.ppermute(msg_b, ("tm", "row"), pairs_b)

    held, bias = pl.pallas_call(
        load_weights,
        out_shape=(shape(3 * LAYER_K, C), shape(3, C, dtype=F32)),
        in_specs=[ANY, ANY],
        out_specs=(VM, VM),
        scratch_shapes=[pltpu.SemaphoreType.DMA((2,))],
        cost_estimate=pl.CostEstimate(flops=0, bytes_accessed=11 << 20, transcendentals=0),
        compiler_params=params(vmem_limit_bytes=36 << 20),
        name="load_weights",
    )(weights, conv_bias)

    tiles = shape(EXT, COLS, T, C)
    side = shape(EXT, 5, T, C)
    lt, ht, left, right, held = pl.pallas_call(
        assemble,
        out_shape=(tiles, tiles, side, side, shape(3 * LAYER_K, C)),
        in_specs=[VM] * 6,
        out_specs=(VM,) * 5,
        input_output_aliases={5: 4},
        scratch_shapes=[
            pltpu.VMEM((14, EXT, COLS, C), BF),
            pltpu.VMEM((4, 16 * COLS, 128), F32),
            pltpu.SemaphoreType.DMA((6,)),
        ],
        compiler_params=params(vmem_limit_bytes=18 << 20),
        name="assemble",
    )(own, other, old, halo_a, halo_b, held)
    from_right = lax.ppermute(left, "col", [(i + 1, i) for i in range(n_col - 1)])
    from_left = lax.ppermute(right, "col", [(i, i + 1) for i in range(n_col - 1)])

    grids = (shape(3, 23, 14, T, C, dtype=F32), shape(3, 21, 12, T, C, dtype=F32),
             shape(3, 19, 10, T, C, dtype=F32))
    past = shape(2, HALF + 1, COLS, C, dtype=F32)
    inner, held, x, y, z, keys, values = pl.pallas_call(
        interior,
        out_shape=(shape(17, 2, T, C), shape(3 * LAYER_K, C)) + grids + (past, past),
        in_specs=[VM] * 8 + [ANY] * 2,
        out_specs=(VM,) * 7,
        input_output_aliases={2: 1},
        scratch_shapes=[pltpu.VMEM((21, 6, T, C), F32)]
        + [pltpu.VMEM((HALF + 1, 2, T, C), F32)] * 4
        + [pltpu.VMEM((2, HALF, COLS, C), BF)] * 2
        + [pltpu.SemaphoreType.DMA((2,))],
        cost_estimate=pl.CostEstimate(
            flops=2 * 1888 * LAYER_K * C, bytes_accessed=14 << 20, transcendentals=0),
        compiler_params=params(vmem_limit_bytes=18 << 20),
        name="interior",
    )(lt, ht, held, bias, w_query, w_key, w_value, w_out, cache_key, cache_value)

    mine, theirs, _, _, _ = pl.pallas_call(
        exterior,
        out_shape=(shape(4, HALF, COLS, C), shape(4, HALF, COLS, C)) + grids,
        in_specs=[VM] * 16,
        out_specs=(VM,) * 5,
        input_output_aliases={11: 2, 12: 3, 13: 4},
        scratch_shapes=[pltpu.VMEM((21, 6, T, C), F32)]
        + [pltpu.VMEM((HALF + 1, 6, T, C), F32)] * 4
        + [pltpu.VMEM((2, HALF * COLS * T, 128), F32)],
        cost_estimate=pl.CostEstimate(
            flops=2 * 3000 * LAYER_K * C, bytes_accessed=18 << 20, transcendentals=0),
        compiler_params=params(vmem_limit_bytes=18 << 20),
        name="exterior",
    )(lt, ht, from_left, from_right, inner, held, bias, w_query, w_key, w_value, w_out, x, y, z,
      keys, values)
    got = lax.ppermute(theirs, "tm", [(0, 1), (1, 0)])
    return pl.pallas_call(
        merge,
        out_shape=shape(4, ROWS, COLS, C),
        in_specs=[VM, VM],
        out_specs=HB,
        scratch_shapes=[pltpu.SemaphoreType.DMA((2,))],
        compiler_params=params(vmem_limit_bytes=30 << 20),
        name="merge",
    )(mine, got)


def solution(mesh):
    return jax.shard_map(
        local,
        mesh=mesh,
        in_specs=(
            P("tm", "row", "col", None),
            P(None, None, "row", "col", None),
            P(),
            P(),
            P(),
            P(),
            P(),
            P(),
            P(None, "row", "col", None),
            P(None, "row", "col", None),
        ),
        out_specs=P("tm", "row", "col", None),
        check_vma=False,
    )
```

time: 85.8 us -> 58 us (0.68)
  the two profiles are of different devices: /device:TPU:131 before, /device:TPU:123 now
where the time goes in v1:
time: 58 us; the launch traced here: 57.8 us
  Pallas kernels  38.5 us (66%)
  starting transfers between devices  13.6 us (23%)
  waiting for transfers between devices  4.76 us (8%)
  local copies, waits for them, and re-layouts  0.72 us (1%)
    pallas_call x1, Pallas kernels, local(): pl.pallas_call(exterior, out_shape=(shape(4, HALF, COLS, C), shape(4, HAL...  19.1 us
    pallas_call x1, Pallas kernels, local(): pl.pallas_call(interior, out_shape=(shape(17, 2, T, C), shape(3 * LAYER_K...  12.3 us
    ppermute x1, starting transfers between devices, local(): lax.ppermute(right, 'col', [(i, i + 1) for i in range(n_col - 1)])  4.42 us
    pallas_call x1, Pallas kernels, local(): pl.pallas_call(load_weights, out_shape=(shape(3 * LAYER_K, C), shape(3, C...  4.03 us
    ppermute x1, starting transfers between devices, local(): halo_b = lax.ppermute(msg_b, ('tm', 'row'), pairs_b)  3.95 us
    ppermute x1, waiting for transfers between devices, local(): lax.ppermute(left, 'col', [(i + 1, i) for i in range(n_col - 1)])  3.57 us
    ppermute x1, starting transfers between devices, local(): halo_a = lax.ppermute(msg_a, ('tm', 'row'), pairs_a)  2.16 us
    ppermute x1, starting transfers between devices, local(): lax.ppermute(left, 'col', [(i + 1, i) for i in range(n_col - 1)])  1.92 us
  transfers between devices with their start and end apart: 6, of which 2 were waited for; matrix products, arithmetic and copies ran while one was open for 0% of the time, Pallas kernels for 31%

profile of v1, /device:TPU:123, one launch (start us, length us, event | category | flops | bytes accessed | tf_op | source)
XLA Modules:
  0.0 57.8 jit_solution(15112026698563049052)
XLA Ops:
  0.0 0.7 %collective-permute-start = (bf16[4,34,8,256]{3,2,1,0:T(8,128)(2,1)}, bf16[4,34,8,256]{3,2,1,0:T(8,128)(2,1)S(1)}, u32[]{:S(2)}, u32[]{:S(2)}) collective-permute-start(bf16[4,34,8,256]{3,2,1,0:T(8,128)(2,1)} %latent.1), channel_id=1, source_target_pairs={{0,128},{128,0},{1,129},{129,1},{2,130},{130,2},{3,131},{131,3},{4... | collective-permute-start | bytes 1671176 | tf_op jit(solution)/shard_map/ppermute | solution.py:365
  0.7 1.3 %pack_rows.1 = (bf16[10,3,8,256]{3,2,1,0:T(8,128)(2,1)S(1)}, bf16[4,3,8,256]{3,2,1,0:T(8,128)(2,1)S(1)}, bf16[4,20,8,256]{3,2,1,0:T(8,128)(2,1)S(1)}, bf16[6,20,8,256]{3,2,1,0:T(8,128)(2,1)S(1)}) custom-call(bf16[4,34,8,256]{3,2,1,0:T(8,128)(2,1)} %latent.1, bf16[6,34,8,256]{3,2,1,0:T(8,128)(2,1)} %bitcast.3), custom_call_target="tpu_custom_call" | custom-call | tf_op jit(solution)/shard_map/pack_rows/pallas_call | solution.py:355
  2.0 2.2 %collective-permute-start.1 = (bf16[10,3,8,256]{3,2,1,0:T(8,128)(2,1)S(1)}, bf16[10,3,8,256]{3,2,1,0:T(8,128)(2,1)S(1)}, u32[]{:S(2)}, u32[]{:S(2)}) collective-permute-start(bf16[10,3,8,256]{3,2,1,0:T(8,128)(2,1)S(1)} %get-tuple-element.27), channel_id=1, source_target_pairs={{0,32},{32,64},{64,96},{160,128},{192,160},{224,192},{1,33},{33,65... | collective-permute-start | bytes 368648 | tf_op jit(solution)/shard_map/ppermute | solution.py:370
  4.1 4.0 %collective-permute-start.2 = (bf16[4,3,8,256]{3,2,1,0:T(8,128)(2,1)S(1)}, bf16[4,3,8,256]{3,2,1,0:T(8,128)(2,1)S(1)}, u32[]{:S(2)}, u32[]{:S(2)}) collective-permute-start(bf16[4,3,8,256]{3,2,1,0:T(8,128)(2,1)S(1)} %get-tuple-element.28), channel_id=1, source_target_pairs={{128,32},{160,64},{192,96},{32,128},{64,160},{96,192},{129,33},{16... | collective-permute-start | bytes 147464 | tf_op jit(solution)/shard_map/ppermute | solution.py:371
  8.1 0.0 copy-start
  8.1 0.7 %copy-done = f32[3,256]{1,0:T(4,128)S(1)} copy-done((f32[3,256]{1,0:T(4,128)S(1)}, f32[3,256]{1,0:T(4,128)}, u32[]{:S(2)}) %copy-start) | copy-done | bytes 3096
  8.8 4.0 %load_weights.1 = (bf16[20736,256]{1,0:T(8,128)(2,1)S(1)}, f32[3,256]{1,0:T(4,128)S(1)}) custom-call(bf16[20736,256]{1,0:T(8,128)(2,1)} %bitcast.2, f32[3,256]{1,0:T(4,128)S(1)} %copy-done), custom_call_target="tpu_custom_call" | custom-call | bytes 11534336 | tf_op jit(solution)/shard_map/load_weights/pallas_call | solution.py:373
  12.8 0.0 copy-start.1
  12.8 0.0 copy-start.2
  12.8 0.0 copy-start.3
  12.8 0.0 copy-start.4
  12.9 0.0 copy-start.5
  12.9 0.0 copy-start.6
  12.9 0.0 collective-permute-done.2.halo_b
  12.9 0.0 collective-permute-done.1.halo_a
  12.9 0.0 collective-permute-done.other
  12.9 1.0 %assemble.1 = (bf16[23,8,8,256]{3,2,1,0:T(8,128)(2,1)S(1)}, bf16[23,8,8,256]{3,2,1,0:T(8,128)(2,1)S(1)}, bf16[23,5,8,256]{3,2,1,0:T(8,128)(2,1)S(1)}, bf16[23,5,...) custom-call(bf16[4,20,8,256]{3,2,1,0:T(8,128)(2,1)S(1)} %get-tuple-element.25.own, ...), custom_call_target="tpu_custom_call", output_to_operand_aliasing={{4}: (5, {})} | custom-call | tf_op jit(solution)/shard_map/assemble/pallas_call | solution.py:386
  13.9 4.4 %collective-permute-start.3 = (bf16[23,5,8,256]{3,2,1,0:T(8,128)(2,1)S(1)}, bf16[23,5,8,256]{3,2,1,0:T(8,128)(2,1)S(1)}, u32[]{:S(2)}, u32[]{:S(2)}) collective-permute-start(bf16[23,5,8,256]{3,2,1,0:T(8,128)(2,1)S(1)} %get-tuple-element.32), channel_id=1, source_target_pairs={{0,1},{1,2},{2,3},{3,4},{4,5},{5,6},{6,7},{7,8},{8,9},{9,10},{10,1... | collective-permute-start | bytes 1413128 | tf_op jit(solution)/shard_map/ppermute | solution.py:401
  18.3 1.9 %collective-permute-start.4 = (bf16[23,5,8,256]{3,2,1,0:T(8,128)(2,1)S(1)}, bf16[23,5,8,256]{3,2,1,0:T(8,128)(2,1)S(1)}, u32[]{:S(2)}, u32[]{:S(2)}) collective-permute-start(bf16[23,5,8,256]{3,2,1,0:T(8,128)(2,1)S(1)} %get-tuple-element.33), channel_id=1, source_target_pairs={{1,0},{2,1},{3,2},{4,3},{5,4},{6,5},{7,6},{8,7},{9,8},{10,9},{11,1... | collective-permute-start | bytes 1413128 | tf_op jit(solution)/shard_map/ppermute | solution.py:400
  20.3 0.0 copy-done.1
  20.3 0.0 copy-done.2
  20.3 0.0 copy-done.3
  20.3 0.0 copy-done.4
  20.3 0.0 copy-done.5
  20.3 0.0 copy-done.6
  20.3 12.3 %interior.1 = (bf16[17,2,8,256]{3,2,1,0:T(8,128)(2,1)S(1)}, bf16[20736,256]{1,0:T(8,128)(2,1)S(1)}, f32[3,23,14,8,256]{4,3,2,1,0:T(8,128)S(1)}, f32[3,21,12,8,25...) custom-call(bf16[23,8,8,256]{3,2,1,0:T(8,128)(2,1)S(1)} %get-tuple-e, ...), custom_call_target="tpu_custom_call", output_to_operand_aliasing={{1}: (2, {})} | custom-call | flops 6681526272 | bytes 14680064 | tf_op jit(solution)/shard_map/interior/pallas_call | solution.py:406
  32.7 0.0 collective-permute-done.3.from_left
  32.7 3.6 %collective-permute-done.4.from_right = bf16[23,5,8,256]{3,2,1,0:T(8,128)(2,1)S(1)} collective-permute-done((bf16[23,5,8,256]{3,2,1,0:T(8,128)(2,1)S(1)}, bf16[23,5,8,256]{3,2,1,0:T(8,128)(2,1)S(1)}, u32[]{:S(2)}, u32[]{:S(2)}) %collective-permute-start.4) | collective-permute-done | bytes 471072 | tf_op jit(solution)/shard_map/ppermute | solution.py:400
  36.2 19.1 %exterior.1 = (bf16[4,17,8,256]{3,2,1,0:T(8,128)(2,1)S(1)}, bf16[4,17,8,256]{3,2,1,0:T(8,128)(2,1)S(1)}, f32[3,23,14,8,256]{4,3,2,1,0:T(8,128)S(1)}, f32[3,21,12...) custom-call(bf16[23,8,8,256]{3,2,1,0:T(8,128)(2,1)S(1)} %get-tuple-e, ...), custom_call_target="tpu_custom_call", output_to_operand_aliasing={{2}: (11, {}), {3}: (12, {}), {4}: (13, {})} | custom-call | flops 10616832000 | bytes 18874368 | tf_op jit(solution)/shard_map/exterior/pallas_call | solution.py:422
  55.3 0.5 collective-permute-start.5
  55.8 1.2 %collective-permute-done.5.got = bf16[4,17,8,256]{3,2,1,0:T(8,128)(2,1)S(1)} collective-permute-done((bf16[4,17,8,256]{3,2,1,0:T(8,128)(2,1)S(1)}, bf16[4,17,8,256]{3,2,1,0:T(8,128)(2,1)S(1)}, u32[]{:S(2)}, u32[]{:S(2)}) %collective-permute-start.5) | collective-permute-done | bytes 278560 | tf_op jit(solution)/shard_map/ppermute | solution.py:437
  57.0 0.8 %merge.1 = bf16[4,34,8,256]{3,2,1,0:T(8,128)(2,1)} custom-call(bf16[4,17,8,256]{3,2,1,0:T(8,128)(2,1)S(1)} %get-tuple-element.43.mine, bf16[4,17,8,256]{3,2,1,0:T(8,128)(2,1)S(1)} %collective-permute-done.5.got), custom_call_target="tpu_custom_call" | custom-call | tf_op jit(solution)/shard_map/merge/pallas_call | solution.py:438
Async XLA Ops:
  0.0 12.9 %collective-permute-start = (bf16[4,34,8,256]{3,2,1,0:T(8,128)(2,1)}, bf16[4,34,8,256]{3,2,1,0:T(8,128)(2,1)S(1)}, u32[]{:S(2)}, u32[]{:S(2)}) collective-permute-start(bf16[4,34,8,256]{3,2,1,0:T(8,128)(2,1)} %latent.1), channel_id=1, source_target_pairs={{0,128},{128,0},{1,129},{129,1},{2,130},{130,2},{3,131},{131,3},{4... | collective-permute-start | bytes 1671176 | tf_op jit(solution)/shard_map/ppermute | solution.py:365
  2.0 10.9 %collective-permute-start.1 = (bf16[10,3,8,256]{3,2,1,0:T(8,128)(2,1)S(1)}, bf16[10,3,8,256]{3,2,1,0:T(8,128)(2,1)S(1)}, u32[]{:S(2)}, u32[]{:S(2)}) collective-permute-start(bf16[10,3,8,256]{3,2,1,0:T(8,128)(2,1)S(1)} %get-tuple-element.27), channel_id=1, source_target_pairs={{0,32},{32,64},{64,96},{160,128},{192,160},{224,192},{1,33},{33,65... | collective-permute-start | bytes 368648 | tf_op jit(solution)/shard_map/ppermute | solution.py:370
  4.1 8.8 %collective-permute-start.2 = (bf16[4,3,8,256]{3,2,1,0:T(8,128)(2,1)S(1)}, bf16[4,3,8,256]{3,2,1,0:T(8,128)(2,1)S(1)}, u32[]{:S(2)}, u32[]{:S(2)}) collective-permute-start(bf16[4,3,8,256]{3,2,1,0:T(8,128)(2,1)S(1)} %get-tuple-element.28), channel_id=1, source_target_pairs={{128,32},{160,64},{192,96},{32,128},{64,160},{96,192},{129,33},{16... | collective-permute-start | bytes 147464 | tf_op jit(solution)/shard_map/ppermute | solution.py:371
  8.1 0.7 %copy-start = (f32[3,256]{1,0:T(4,128)S(1)}, f32[3,256]{1,0:T(4,128)}, u32[]{:S(2)}) copy-start(f32[3,256]{1,0:T(4,128)} %bias.1) | copy-start | bytes 9220
  12.8 7.4 %copy-start.1 = (bf16[2,34,8,256]{3,2,1,0:T(8,128)(2,1)S(1)}, bf16[2,34,8,256]{3,2,1,0:T(8,128)(2,1)}, u32[]{:S(2)}) copy-start(bf16[2,34,8,256]{3,2,1,0:T(8,128)(2,1)} %key_cache.1) | copy-start | bytes 835588
  12.8 7.4 %copy-start.2 = (bf16[2,34,8,256]{3,2,1,0:T(8,128)(2,1)S(1)}, bf16[2,34,8,256]{3,2,1,0:T(8,128)(2,1)}, u32[]{:S(2)}) copy-start(bf16[2,34,8,256]{3,2,1,0:T(8,128)(2,1)} %value_cache.1) | copy-start | bytes 835588
  12.8 7.4 %copy-start.3 = (bf16[256,256]{1,0:T(8,128)(2,1)S(1)}, bf16[256,256]{1,0:T(8,128)(2,1)}, u32[]{:S(2)}) copy-start(bf16[256,256]{1,0:T(8,128)(2,1)} %wq.3) | copy-start | bytes 393220
  12.8 7.4 %copy-start.4 = (bf16[256,256]{1,0:T(8,128)(2,1)S(1)}, bf16[256,256]{1,0:T(8,128)(2,1)}, u32[]{:S(2)}) copy-start(bf16[256,256]{1,0:T(8,128)(2,1)} %wk.3) | copy-start | bytes 393220
  12.9 7.4 %copy-start.5 = (bf16[256,256]{1,0:T(8,128)(2,1)S(1)}, bf16[256,256]{1,0:T(8,128)(2,1)}, u32[]{:S(2)}) copy-start(bf16[256,256]{1,0:T(8,128)(2,1)} %wv.3) | copy-start | bytes 393220
  12.9 7.4 %copy-start.6 = (bf16[256,256]{1,0:T(8,128)(2,1)S(1)}, bf16[256,256]{1,0:T(8,128)(2,1)}, u32[]{:S(2)}) copy-start(bf16[256,256]{1,0:T(8,128)(2,1)} %wo.3) | copy-start | bytes 393220
  13.9 18.8 %collective-permute-start.3 = (bf16[23,5,8,256]{3,2,1,0:T(8,128)(2,1)S(1)}, bf16[23,5,8,256]{3,2,1,0:T(8,128)(2,1)S(1)}, u32[]{:S(2)}, u32[]{:S(2)}) collective-permute-start(bf16[23,5,8,256]{3,2,1,0:T(8,128)(2,1)S(1)} %get-tuple-element.32), channel_id=1, source_target_pairs={{0,1},{1,2},{2,3},{3,4},{4,5},{5,6},{6,7},{7,8},{8,9},{9,10},{10,1... | collective-permute-start | bytes 1413128 | tf_op jit(solution)/shard_map/ppermute | solution.py:401
  18.3 17.9 %collective-permute-start.4 = (bf16[23,5,8,256]{3,2,1,0:T(8,128)(2,1)S(1)}, bf16[23,5,8,256]{3,2,1,0:T(8,128)(2,1)S(1)}, u32[]{:S(2)}, u32[]{:S(2)}) collective-permute-start(bf16[23,5,8,256]{3,2,1,0:T(8,128)(2,1)S(1)} %get-tuple-element.33), channel_id=1, source_target_pairs={{1,0},{2,1},{3,2},{4,3},{5,4},{6,5},{7,6},{8,7},{9,8},{10,9},{11,1... | collective-permute-start | bytes 1413128 | tf_op jit(solution)/shard_map/ppermute | solution.py:400
  55.3 1.7 %collective-permute-start.5 = (bf16[4,17,8,256]{3,2,1,0:T(8,128)(2,1)S(1)}, bf16[4,17,8,256]{3,2,1,0:T(8,128)(2,1)S(1)}, u32[]{:S(2)}, u32[]{:S(2)}) collective-permute-start(bf16[4,17,8,256]{3,2,1,0:T(8,128)(2,1)S(1)} %get-tuple-element.44), channel_id=1, source_target_pairs={{0,128},{128,0},{1,129},{129,1},{2,130},{130,2},{3,131},{131,3},{4... | collective-permute-start | bytes 835592 | tf_op jit(solution)/shard_map/ppermute | solution.py:437

commit v2 on v1

--- a/solution.py
+++ b/solution.py
@@ -49,11 +49,9 @@
     ])
 
 
-def load_weights(weights, bias, held, held_bias, sems):
-    run_copies([
-        pltpu.make_async_copy(weights, held, sems.at[0]),
-        pltpu.make_async_copy(bias, held_bias, sems.at[1]),
-    ])
+def load_first(weights, held, sems):
+    run_copies([pltpu.make_async_copy(
+        weights.at[0:LAYER_K], held.at[0:LAYER_K], sems.at[0])])
 
 
 def assemble(own, other, cache, halo_a, halo_b, held, lt, ht, left, right, kept, stage, wide, sems):
@@ -118,34 +116,55 @@
         k %= T
         return v if k == 0 else pltpu.roll(v, k, 1)
 
-    dst[2, r, at:at + n] = now
-    dst[1, r, at:at + n] = jnp.where(sub < 1, roll(past, -2 * layer - 1), roll(now, 1))
-    dst[0, r, at:at + n] = jnp.where(sub < 2, roll(past, -2 * layer), roll(now, 2))
-
-
-def conv(src, rows, groups, held, layer, bias, dst):
+    tile, odd = r // 2, r % 2
+    dst[2, tile, odd, at:at + n] = now
+    dst[1, tile, odd, at:at + n] = jnp.where(sub < 1, roll(past, -2 * layer - 1), roll(now, 1))
+    dst[0, tile, odd, at:at + n] = jnp.where(sub < 2, roll(past, -2 * layer), roll(now, 2))
+
+
+def conv(src, tiles, groups, held, layer, bias, dst):
     count = sum(n for _, n in groups)
-    step = (rows + 1) // 2
-
-    def body(i, carry):
-        r = i * (rows - step)
+
+    def block(a, k, c):
+        def rows(shift, odd):
+            cols = [src[a, shift:shift + tiles, odd, first + c:first + c + n]
+                    for first, n in groups]
+            return cols[0] if len(cols) == 1 else jnp.concatenate(cols, 1)
+
+        if k == 0:
+            v = rows(0, 0) - rows(1, 0)
+        elif k == 1:
+            v = rows(0, 1) + rows(1, 0)
+        elif k == 2:
+            v = rows(1, 0) - rows(0, 1)
+        else:
+            v = rows(0, 1) - rows(1, 1)
+        return v.reshape(tiles * count * T, C).astype(BF)
+
+    def weight(a, k):
+        def taps(b):
+            at = layer * LAYER_K + (a * 3 + b) * 3 * C
+            return held[at:at + 3 * C]
+
+        if k in (0, 3):
+            return taps(0 if k == 0 else 2)
+        outer = (taps(0).astype(F32) + taps(2).astype(F32)) * 0.5
+        inner = taps(1).astype(F32) * 0.5
+        return (outer + inner if k == 1 else outer - inner).astype(BF)
+
+    def product(k):
         total = None
         for a in range(3):
-            for b in range(3):
-                parts = []
-                for c in range(3):
-                    cols = [src[a, pl.ds(r + b, step), first + c:first + c + n]
-                            for first, n in groups]
-                    block = cols[0] if len(cols) == 1 else jnp.concatenate(cols, 1)
-                    parts.append(block.reshape(step * count * T, C).astype(BF))
-                k = layer * LAYER_K + (a * 3 + b) * 3 * C
-                part = jnp.dot(
-                    jnp.concatenate(parts, 1), held[k:k + 3 * C], preferred_element_type=F32)
-                total = part if total is None else total + part
-        dst[pl.ds(r, step), 0:count] = (total + bias).reshape(step, count, T, C)
-        return carry
-
-    lax.fori_loop(0, 2, body, 0)
+            part = jnp.dot(jnp.concatenate([block(a, k, c) for c in range(3)], 1),
+                           weight(a, k), preferred_element_type=F32)
+            total = part if total is None else total + part
+        return total
+
+    middle, other = product(1), product(2)
+    even = product(0) + (middle + other) + bias
+    dst[0:tiles, 0, 0:count] = even.reshape(tiles, count, T, C)
+    odd = (middle - other) - product(3) + bias
+    dst[0:tiles, 1, 0:count] = odd.reshape(tiles, count, T, C)
 
 
 def silu(v):
@@ -212,13 +231,17 @@
     return hidden + jnp.dot(mixed, wo[...], preferred_element_type=F32)
 
 
-def interior(lt, ht, held, bias, wq, wk, wv, wo, key_cache, value_cache, out, kept, x, y, z,
+def interior(lt, ht, first, bias, wq, wk, wv, wo, key_cache, value_cache, weights, out, held, x, y, z,
              keys, values, res, qs, ks, vs, mix, ck, cv, sems):
-    del kept
+    del first
     half = lax.axis_index("tm")
     copies = [
         pltpu.make_async_copy(key_cache.at[:, pl.ds(HALF * half, HALF)], ck, sems.at[0]),
         pltpu.make_async_copy(value_cache.at[:, pl.ds(HALF * half, HALF)], cv, sems.at[1]),
+        pltpu.make_async_copy(weights.at[LAYER_K:2 * LAYER_K], held.at[LAYER_K:2 * LAYER_K],
+                              sems.at[2]),
+        pltpu.make_async_copy(weights.at[2 * LAYER_K:3 * LAYER_K],
+                              held.at[2 * LAYER_K:3 * LAYER_K], sems.at[3]),
     ]
     for copy in copies:
         copy.start()
@@ -227,28 +250,30 @@
         put(x, r, 3, lt[r].astype(F32), ht[r].astype(F32), 0)
         return carry
 
-    lax.fori_loop(0, EXT, fill, 0)
-    conv(x, 21, [(3, 6)], held, 0, bias[0:1], res)
+    lax.fori_loop(0, EXT, fill, 0, unroll=2)
+    conv(x, 11, [(3, 6)], held, 0, bias[0:1], res)
     low, high = row_limits(2)
 
     def one(r, carry):
-        v = jnp.where((r >= low) & (r < high), silu(res[r]), 0.0).astype(BF)
+        v = jnp.where((r >= low) & (r < high), silu(res[r // 2, r % 2]), 0.0).astype(BF)
         put(y, r, 3, v.astype(F32), ht[r + 1, 1:7].astype(F32), 1)
         return carry
 
-    lax.fori_loop(0, 21, one, 0)
-    conv(y, 19, [(3, 4)], held, 1, bias[1:2], res)
+    lax.fori_loop(0, 21, one, 0, unroll=3)
+    copies[2].wait()
+    conv(y, 10, [(3, 4)], held, 1, bias[1:2], res)
     low2, high2 = row_limits(1)
 
     def two(r, carry):
-        v = jnp.where((r >= low2) & (r < high2), silu(res[r, 0:4]), 0.0).astype(BF)
+        v = jnp.where((r >= low2) & (r < high2), silu(res[r // 2, r % 2, 0:4]), 0.0).astype(BF)
         put(z, r, 3, v.astype(F32), ht[r + 2, 2:6].astype(F32), 2)
         return carry
 
-    lax.fori_loop(0, 19, two, 0)
-    conv(z, 17, [(3, 2)], held, 2, bias[2:3], res)
-    hidden = (res[0:17, 0:2] + lt[3:20, 3:5].astype(F32)).astype(BF).astype(F32)
-    for copy in copies:
+    lax.fori_loop(0, 19, two, 0, unroll=2)
+    copies[3].wait()
+    conv(z, 9, [(3, 2)], held, 2, bias[2:3], res)
+    hidden = (res[0:9, :, 0:2].reshape(18, 2, T, C)[0:17] + lt[3:20, 3:5].astype(F32)).astype(BF).astype(F32)
+    for copy in copies[0:2]:
         copy.wait()
     for src, dst in ((ck, keys), (cv, values)):
         dst[:, 0:HALF] = src[...].astype(F32)
@@ -276,13 +301,13 @@
             put(x, r, at, side[r, 0:3].astype(F32), past, 0)
         return carry
 
-    lax.fori_loop(0, EXT, fill, 0)
-    conv(x, 21, [(0, 3), (9, 3)], held, 0, bias[0:1], res)
+    lax.fori_loop(0, EXT, fill, 0, unroll=2)
+    conv(x, 11, [(0, 3), (9, 3)], held, 0, bias[0:1], res)
     low, high = row_limits(2)
 
     def one(r, carry):
         ok = (r >= low) & (r < high)
-        v = silu(res[r]).astype(BF).astype(F32)
+        v = silu(res[r // 2, r % 2]).astype(BF).astype(F32)
         e = r + 1
         put(y, r, 0, jnp.concatenate(
             [jnp.where(ok & has_left, v[0:2], 0.0), jnp.where(ok, v[2:3], 0.0)], 0),
@@ -294,13 +319,13 @@
                              from_right[e, 4:5].astype(F32)], 0), 1)
         return carry
 
-    lax.fori_loop(0, 21, one, 0)
-    conv(y, 19, [(0, 3), (7, 3)], held, 1, bias[1:2], res)
+    lax.fori_loop(0, 21, one, 0, unroll=3)
+    conv(y, 10, [(0, 3), (7, 3)], held, 1, bias[1:2], res)
     low2, high2 = row_limits(1)
 
     def two(r, carry):
         ok = (r >= low2) & (r < high2)
-        v = silu(res[r]).astype(BF).astype(F32)
+        v = silu(res[r // 2, r % 2]).astype(BF).astype(F32)
         e = r + 2
         put(z, r, 0, jnp.concatenate(
             [jnp.where(ok & has_left, v[0:1], 0.0), jnp.where(ok, v[1:3], 0.0)], 0),
@@ -310,11 +335,11 @@
             jnp.concatenate([ht[e, 6:8].astype(F32), from_right[e, 3:4].astype(F32)], 0), 2)
         return carry
 
-    lax.fori_loop(0, 19, two, 0)
-    conv(z, 17, [(0, 3), (5, 3)], held, 2, bias[2:3], res)
+    lax.fori_loop(0, 19, two, 0, unroll=2)
+    conv(z, 9, [(0, 3), (5, 3)], held, 2, bias[2:3], res)
     cols = (0, 1, 2, 5, 6, 7)
     own = jnp.concatenate([lt[3:20, 0:3], lt[3:20, 5:8]], 1).astype(F32)
-    hidden = (res[0:17] + own).astype(BF).astype(F32)
+    hidden = (res[0:9].reshape(18, 6, T, C)[0:17] + own).astype(BF).astype(F32)
     done = attend_all(hidden.reshape(HALF * 6 * T, C), cols, 3, wq, wk, wv, wo, keys, values,
                       qs, ks, vs, mix).reshape(HALF, 6, T, C)
     done = jnp.concatenate([done[:, 0:3], inner[...].astype(F32), done[:, 3:6]], 1)
@@ -370,16 +395,16 @@
     halo_a = lax.ppermute(msg_a, ("tm", "row"), pairs_a)
     halo_b = lax.ppermute(msg_b, ("tm", "row"), pairs_b)
 
-    held, bias = pl.pallas_call(
-        load_weights,
-        out_shape=(shape(3 * LAYER_K, C), shape(3, C, dtype=F32)),
-        in_specs=[ANY, ANY],
-        out_specs=(VM, VM),
-        scratch_shapes=[pltpu.SemaphoreType.DMA((2,))],
-        cost_estimate=pl.CostEstimate(flops=0, bytes_accessed=11 << 20, transcendentals=0),
+    held = pl.pallas_call(
+        load_first,
+        out_shape=shape(3 * LAYER_K, C),
+        in_specs=[ANY],
+        out_specs=VM,
+        scratch_shapes=[pltpu.SemaphoreType.DMA((1,))],
+        cost_estimate=pl.CostEstimate(flops=0, bytes_accessed=4 << 20, transcendentals=0),
         compiler_params=params(vmem_limit_bytes=36 << 20),
         name="load_weights",
-    )(weights, conv_bias)
+    )(weights)
 
     tiles = shape(EXT, COLS, T, C)
     side = shape(EXT, 5, T, C)
@@ -394,30 +419,30 @@
             pltpu.VMEM((4, 16 * COLS, 128), F32),
             pltpu.SemaphoreType.DMA((6,)),
         ],
-        compiler_params=params(vmem_limit_bytes=18 << 20),
+        compiler_params=params(vmem_limit_bytes=16 << 20),
         name="assemble",
     )(own, other, old, halo_a, halo_b, held)
     from_right = lax.ppermute(left, "col", [(i + 1, i) for i in range(n_col - 1)])
     from_left = lax.ppermute(right, "col", [(i, i + 1) for i in range(n_col - 1)])
 
-    grids = (shape(3, 23, 14, T, C, dtype=F32), shape(3, 21, 12, T, C, dtype=F32),
-             shape(3, 19, 10, T, C, dtype=F32))
+    grids = (shape(3, 12, 2, 14, T, C, dtype=F32), shape(3, 11, 2, 12, T, C, dtype=F32),
+             shape(3, 10, 2, 10, T, C, dtype=F32))
     past = shape(2, HALF + 1, COLS, C, dtype=F32)
     inner, held, x, y, z, keys, values = pl.pallas_call(
         interior,
         out_shape=(shape(17, 2, T, C), shape(3 * LAYER_K, C)) + grids + (past, past),
-        in_specs=[VM] * 8 + [ANY] * 2,
+        in_specs=[VM] * 8 + [ANY] * 3,
         out_specs=(VM,) * 7,
         input_output_aliases={2: 1},
-        scratch_shapes=[pltpu.VMEM((21, 6, T, C), F32)]
+        scratch_shapes=[pltpu.VMEM((11, 2, 6, T, C), F32)]
         + [pltpu.VMEM((HALF + 1, 2, T, C), F32)] * 4
         + [pltpu.VMEM((2, HALF, COLS, C), BF)] * 2
-        + [pltpu.SemaphoreType.DMA((2,))],
+        + [pltpu.SemaphoreType.DMA((4,))],
         cost_estimate=pl.CostEstimate(
             flops=2 * 1888 * LAYER_K * C, bytes_accessed=14 << 20, transcendentals=0),
-        compiler_params=params(vmem_limit_bytes=18 << 20),
+        compiler_params=params(vmem_limit_bytes=16 << 20),
         name="interior",
-    )(lt, ht, held, bias, w_query, w_key, w_value, w_out, cache_key, cache_value)
+    )(lt, ht, held, conv_bias, w_query, w_key, w_value, w_out, cache_key, cache_value, weights)
 
     mine, theirs, _, _, _ = pl.pallas_call(
         exterior,
@@ -425,14 +450,14 @@
         in_specs=[VM] * 16,
         out_specs=(VM,) * 5,
         input_output_aliases={11: 2, 12: 3, 13: 4},
-        scratch_shapes=[pltpu.VMEM((21, 6, T, C), F32)]
+        scratch_shapes=[pltpu.VMEM((11, 2, 6, T, C), F32)]
         + [pltpu.VMEM((HALF + 1, 6, T, C), F32)] * 4
         + [pltpu.VMEM((2, HALF * COLS * T, 128), F32)],
         cost_estimate=pl.CostEstimate(
             flops=2 * 3000 * LAYER_K * C, bytes_accessed=18 << 20, transcendentals=0),
-        compiler_params=params(vmem_limit_bytes=18 << 20),
+        compiler_params=params(vmem_limit_bytes=16 << 20),
         name="exterior",
-    )(lt, ht, from_left, from_right, inner, held, bias, w_query, w_key, w_value, w_out, x, y, z,
+    )(lt, ht, from_left, from_right, inner, held, conv_bias, w_query, w_key, w_value, w_out, x, y, z,
       keys, values)
     got = lax.ppermute(theirs, "tm", [(0, 1), (1, 0)])
     return pl.pallas_call(

time: 58 us -> 52.8 us (0.910)
  Pallas kernels: 38.5 us -> 32.3 us
  starting transfers between devices: 13.6 us -> 14.9 us
  local copies, waits for them, and re-layouts: 0.72 us -> 0.04 us
    pallas_call x1, Pallas kernels: 19.1 us -> 16.2 us  [local(): pl.pallas_call(exterior, out_shape=(shape(4, HALF, COLS, C), shape(4, HAL...]
    pallas_call x1, Pallas kernels: 4.03 us -> 2.01 us  [local(): pl.pallas_call(load_first, out_shape=shape(3 * LAYER_K, C), in_specs=[ANY...]
    ppermute x1, starting transfers between devices: 0.48 us -> 1.8 us  [local(): got = lax.ppermute(theirs, 'tm', [(0, 1), (1, 0)])]
    pallas_call x1, Pallas kernels: 12.3 us -> 11 us  [local(): pl.pallas_call(interior, out_shape=(shape(17, 2, T, C), shape(3 * LAYER_K...]
    unnamed x14, local copies, waits for them, and re-layouts: 0.72 us -> 0.04 us
  transfers between devices with their start and end apart: 6 -> 6, of which waited for: 2 -> 2; matrix products, arithmetic and copies ran while one was open for 0% -> 0% of each run, Pallas kernels for 31% -> 27%
where the time goes in v2:
time: 52.8 us; the launch traced here: 52.5 us
  Pallas kernels  32.3 us (61%)
  starting transfers between devices  14.9 us (28%)
  waiting for transfers between devices  4.86 us (9%)
    pallas_call x1, Pallas kernels, local(): pl.pallas_call(exterior, out_shape=(shape(4, HALF, COLS, C), shape(4, HAL...  16.2 us
    pallas_call x1, Pallas kernels, local(): pl.pallas_call(interior, out_shape=(shape(17, 2, T, C), shape(3 * LAYER_K...  11 us
    ppermute x1, starting transfers between devices, local(): lax.ppermute(right, 'col', [(i, i + 1) for i in range(n_col - 1)])  4.42 us
    ppermute x1, starting transfers between devices, local(): halo_b = lax.ppermute(msg_b, ('tm', 'row'), pairs_b)  3.95 us
    ppermute x1, waiting for transfers between devices, local(): lax.ppermute(left, 'col', [(i + 1, i) for i in range(n_col - 1)])  3.66 us
    ppermute x1, starting transfers between devices, local(): halo_a = lax.ppermute(msg_a, ('tm', 'row'), pairs_a)  2.16 us
    pallas_call x1, Pallas kernels, local(): pl.pallas_call(load_first, out_shape=shape(3 * LAYER_K, C), in_specs=[ANY...  2.01 us
    ppermute x1, starting transfers between devices, local(): lax.ppermute(left, 'col', [(i + 1, i) for i in range(n_col - 1)])  1.92 us
  transfers between devices with their start and end apart: 6, of which 2 were waited for; matrix products, arithmetic and copies ran while one was open for 0% of the time, Pallas kernels for 27%

profile of v2, /device:TPU:123, one launch (start us, length us, event | category | flops | bytes accessed | tf_op | source)
XLA Modules:
  0.0 52.5 jit_solution(18184388341056081003)
XLA Ops:
  0.0 0.7 %collective-permute-start = (bf16[4,34,8,256]{3,2,1,0:T(8,128)(2,1)}, bf16[4,34,8,256]{3,2,1,0:T(8,128)(2,1)S(1)}, u32[]{:S(2)}, u32[]{:S(2)}) collective-permute-start(bf16[4,34,8,256]{3,2,1,0:T(8,128)(2,1)} %latent.1), channel_id=1, source_target_pairs={{0,128},{128,0},{1,129},{129,1},{2,130},{130,2},{3,131},{131,3},{4... | collective-permute-start | bytes 1671176 | tf_op jit(solution)/shard_map/ppermute | solution.py:390
  0.7 1.3 %pack_rows.1 = (bf16[10,3,8,256]{3,2,1,0:T(8,128)(2,1)S(1)}, bf16[4,3,8,256]{3,2,1,0:T(8,128)(2,1)S(1)}, bf16[4,20,8,256]{3,2,1,0:T(8,128)(2,1)S(1)}, bf16[6,20,8,256]{3,2,1,0:T(8,128)(2,1)S(1)}) custom-call(bf16[4,34,8,256]{3,2,1,0:T(8,128)(2,1)} %latent.1, bf16[6,34,8,256]{3,2,1,0:T(8,128)(2,1)} %bitcast.4), custom_call_target="tpu_custom_call" | custom-call | tf_op jit(solution)/shard_map/pack_rows/pallas_call | solution.py:380
  2.0 2.2 %collective-permute-start.1 = (bf16[10,3,8,256]{3,2,1,0:T(8,128)(2,1)S(1)}, bf16[10,3,8,256]{3,2,1,0:T(8,128)(2,1)S(1)}, u32[]{:S(2)}, u32[]{:S(2)}) collective-permute-start(bf16[10,3,8,256]{3,2,1,0:T(8,128)(2,1)S(1)} %get-tuple-element.25), channel_id=1, source_target_pairs={{0,32},{32,64},{64,96},{160,128},{192,160},{224,192},{1,33},{33,65... | collective-permute-start | bytes 368648 | tf_op jit(solution)/shard_map/ppermute | solution.py:395
  4.1 4.0 %collective-permute-start.2 = (bf16[4,3,8,256]{3,2,1,0:T(8,128)(2,1)S(1)}, bf16[4,3,8,256]{3,2,1,0:T(8,128)(2,1)S(1)}, u32[]{:S(2)}, u32[]{:S(2)}) collective-permute-start(bf16[4,3,8,256]{3,2,1,0:T(8,128)(2,1)S(1)} %get-tuple-element.26), channel_id=1, source_target_pairs={{128,32},{160,64},{192,96},{32,128},{64,160},{96,192},{129,33},{16... | collective-permute-start | bytes 147464 | tf_op jit(solution)/shard_map/ppermute | solution.py:396
  8.1 2.0 %load_weights.1.held = bf16[20736,256]{1,0:T(8,128)(2,1)S(1)} custom-call(bf16[20736,256]{1,0:T(8,128)(2,1)} %bitcast.2), custom_call_target="tpu_custom_call" | custom-call | bytes 4194304 | tf_op jit(solution)/shard_map/load_weights/pallas_call | solution.py:398
  10.1 0.0 copy-start
  10.1 0.0 copy-start.1
  10.1 0.0 copy-start.2
  10.1 0.0 copy-start.3
  10.2 0.0 copy-start.4
  10.2 0.0 copy-start.5
  10.2 0.0 copy-start.6
  10.2 0.0 collective-permute-done.2.halo_b
  10.2 0.0 collective-permute-done.1.halo_a
  10.2 0.0 collective-permute-done.other
  10.2 1.0 %assemble.1 = (bf16[23,8,8,256]{3,2,1,0:T(8,128)(2,1)S(1)}, bf16[23,8,8,256]{3,2,1,0:T(8,128)(2,1)S(1)}, bf16[23,5,8,256]{3,2,1,0:T(8,128)(2,1)S(1)}, bf16[23,5,...) custom-call(bf16[4,20,8,256]{3,2,1,0:T(8,128)(2,1)S(1)} %get-tuple-element.23.own, ...), custom_call_target="tpu_custom_call", output_to_operand_aliasing={{4}: (5, {})} | custom-call | tf_op jit(solution)/shard_map/assemble/pallas_call | solution.py:411
  11.2 4.4 %collective-permute-start.3 = (bf16[23,5,8,256]{3,2,1,0:T(8,128)(2,1)S(1)}, bf16[23,5,8,256]{3,2,1,0:T(8,128)(2,1)S(1)}, u32[]{:S(2)}, u32[]{:S(2)}) collective-permute-start(bf16[23,5,8,256]{3,2,1,0:T(8,128)(2,1)S(1)} %get-tuple-element.29), channel_id=1, source_target_pairs={{0,1},{1,2},{2,3},{3,4},{4,5},{5,6},{6,7},{7,8},{8,9},{9,10},{10,1... | collective-permute-start | bytes 1413128 | tf_op jit(solution)/shard_map/ppermute | solution.py:426
  15.6 1.9 %collective-permute-start.4 = (bf16[23,5,8,256]{3,2,1,0:T(8,128)(2,1)S(1)}, bf16[23,5,8,256]{3,2,1,0:T(8,128)(2,1)S(1)}, u32[]{:S(2)}, u32[]{:S(2)}) collective-permute-start(bf16[23,5,8,256]{3,2,1,0:T(8,128)(2,1)S(1)} %get-tuple-element.30), channel_id=1, source_target_pairs={{1,0},{2,1},{3,2},{4,3},{5,4},{6,5},{7,6},{8,7},{9,8},{10,9},{11,1... | collective-permute-start | bytes 1413128 | tf_op jit(solution)/shard_map/ppermute | solution.py:425
  17.6 0.0 copy-done
  17.6 0.0 copy-done.1
  17.6 0.0 copy-done.2
  17.6 0.0 copy-done.3
  17.6 0.0 copy-done.4
  17.6 0.0 copy-done.5
  17.6 0.0 copy-done.6
  17.6 11.0 %interior.1 = (bf16[17,2,8,256]{3,2,1,0:T(8,128)(2,1)S(1)}, bf16[20736,256]{1,0:T(8,128)(2,1)S(1)}, f32[3,12,2,14,8,256]{5,4,3,2,1,0:T(8,128)S(1)}, f32[3,11,2,1...) custom-call(bf16[23,8,8,256]{3,2,1,0:T(8,128)(2,1)S(1)} %get-tuple-e, ...), custom_call_target="tpu_custom_call", output_to_operand_aliasing={{1}: (2, {})} | custom-call | flops 6681526272 | bytes 14680064 | tf_op jit(solution)/shard_map/interior/pallas_call | solution.py:431
  28.6 0.0 collective-permute-done.3.from_left
  28.7 3.7 %collective-permute-done.4.from_right = bf16[23,5,8,256]{3,2,1,0:T(8,128)(2,1)S(1)} collective-permute-done((bf16[23,5,8,256]{3,2,1,0:T(8,128)(2,1)S(1)}, bf16[23,5,8,256]{3,2,1,0:T(8,128)(2,1)S(1)}, u32[]{:S(2)}, u32[]{:S(2)}) %collective-permute-start.4) | collective-permute-done | bytes 471072 | tf_op jit(solution)/shard_map/ppermute | solution.py:425
  32.3 16.2 %exterior.1 = (bf16[4,17,8,256]{3,2,1,0:T(8,128)(2,1)S(1)}, bf16[4,17,8,256]{3,2,1,0:T(8,128)(2,1)S(1)}, f32[3,12,2,14,8,256]{5,4,3,2,1,0:T(8,128)S(1)}, f32[3,1...) custom-call(bf16[23,8,8,256]{3,2,1,0:T(8,128)(2,1)S(1)} %get-tuple-e, ...), custom_call_target="tpu_custom_call", output_to_operand_aliasing={{2}: (11, {}), {3}: (12, {}), {4}: (13, {})} | custom-call | flops 10616832000 | bytes 18874368 | tf_op jit(solution)/shard_map/exterior/pallas_call | solution.py:447
  48.6 1.8 %collective-permute-start.5 = (bf16[4,17,8,256]{3,2,1,0:T(8,128)(2,1)S(1)}, bf16[4,17,8,256]{3,2,1,0:T(8,128)(2,1)S(1)}, u32[]{:S(2)}, u32[]{:S(2)}) collective-permute-start(bf16[4,17,8,256]{3,2,1,0:T(8,128)(2,1)S(1)} %get-tuple-element.40), channel_id=1, source_target_pairs={{0,128},{128,0},{1,129},{129,1},{2,130},{130,2},{3,131},{131,3},{4... | collective-permute-start | bytes 835592 | tf_op jit(solution)/shard_map/ppermute | solution.py:462
  50.4 1.2 %collective-permute-done.5.got = bf16[4,17,8,256]{3,2,1,0:T(8,128)(2,1)S(1)} collective-permute-done((bf16[4,17,8,256]{3,2,1,0:T(8,128)(2,1)S(1)}, bf16[4,17,8,256]{3,2,1,0:T(8,128)(2,1)S(1)}, u32[]{:S(2)}, u32[]{:S(2)}) %collective-permute-start.5) | collective-permute-done | bytes 278560 | tf_op jit(solution)/shard_map/ppermute | solution.py:462
  51.6 0.8 %merge.1 = bf16[4,34,8,256]{3,2,1,0:T(8,128)(2,1)} custom-call(bf16[4,17,8,256]{3,2,1,0:T(8,128)(2,1)S(1)} %get-tuple-element.39.mine, bf16[4,17,8,256]{3,2,1,0:T(8,128)(2,1)S(1)} %collective-permute-done.5.got), custom_call_target="tpu_custom_call" | custom-call | tf_op jit(solution)/shard_map/merge/pallas_call | solution.py:463
Async XLA Ops:
  0.0 10.2 %collective-permute-start = (bf16[4,34,8,256]{3,2,1,0:T(8,128)(2,1)}, bf16[4,34,8,256]{3,2,1,0:T(8,128)(2,1)S(1)}, u32[]{:S(2)}, u32[]{:S(2)}) collective-permute-start(bf16[4,34,8,256]{3,2,1,0:T(8,128)(2,1)} %latent.1), channel_id=1, source_target_pairs={{0,128},{128,0},{1,129},{129,1},{2,130},{130,2},{3,131},{131,3},{4... | collective-permute-start | bytes 1671176 | tf_op jit(solution)/shard_map/ppermute | solution.py:390
  2.0 8.2 %collective-permute-start.1 = (bf16[10,3,8,256]{3,2,1,0:T(8,128)(2,1)S(1)}, bf16[10,3,8,256]{3,2,1,0:T(8,128)(2,1)S(1)}, u32[]{:S(2)}, u32[]{:S(2)}) collective-permute-start(bf16[10,3,8,256]{3,2,1,0:T(8,128)(2,1)S(1)} %get-tuple-element.25), channel_id=1, source_target_pairs={{0,32},{32,64},{64,96},{160,128},{192,160},{224,192},{1,33},{33,65... | collective-permute-start | bytes 368648 | tf_op jit(solution)/shard_map/ppermute | solution.py:395
  4.1 6.1 %collective-permute-start.2 = (bf16[4,3,8,256]{3,2,1,0:T(8,128)(2,1)S(1)}, bf16[4,3,8,256]{3,2,1,0:T(8,128)(2,1)S(1)}, u32[]{:S(2)}, u32[]{:S(2)}) collective-permute-start(bf16[4,3,8,256]{3,2,1,0:T(8,128)(2,1)S(1)} %get-tuple-element.26), channel_id=1, source_target_pairs={{128,32},{160,64},{192,96},{32,128},{64,160},{96,192},{129,33},{16... | collective-permute-start | bytes 147464 | tf_op jit(solution)/shard_map/ppermute | solution.py:396
  10.1 7.5 %copy-start = (bf16[2,34,8,256]{3,2,1,0:T(8,128)(2,1)S(1)}, bf16[2,34,8,256]{3,2,1,0:T(8,128)(2,1)}, u32[]{:S(2)}) copy-start(bf16[2,34,8,256]{3,2,1,0:T(8,128)(2,1)} %key_cache.1) | copy-start | bytes 835588
  10.1 7.5 %copy-start.1 = (bf16[2,34,8,256]{3,2,1,0:T(8,128)(2,1)S(1)}, bf16[2,34,8,256]{3,2,1,0:T(8,128)(2,1)}, u32[]{:S(2)}) copy-start(bf16[2,34,8,256]{3,2,1,0:T(8,128)(2,1)} %value_cache.1) | copy-start | bytes 835588
  10.1 7.4 %copy-start.2 = (bf16[256,256]{1,0:T(8,128)(2,1)S(1)}, bf16[256,256]{1,0:T(8,128)(2,1)}, u32[]{:S(2)}) copy-start(bf16[256,256]{1,0:T(8,128)(2,1)} %wq.3) | copy-start | bytes 393220
  10.1 7.4 %copy-start.3 = (bf16[256,256]{1,0:T(8,128)(2,1)S(1)}, bf16[256,256]{1,0:T(8,128)(2,1)}, u32[]{:S(2)}) copy-start(bf16[256,256]{1,0:T(8,128)(2,1)} %wk.3) | copy-start | bytes 393220
  10.2 7.4 %copy-start.4 = (bf16[256,256]{1,0:T(8,128)(2,1)S(1)}, bf16[256,256]{1,0:T(8,128)(2,1)}, u32[]{:S(2)}) copy-start(bf16[256,256]{1,0:T(8,128)(2,1)} %wv.3) | copy-start | bytes 393220
  10.2 7.4 %copy-start.5 = (bf16[256,256]{1,0:T(8,128)(2,1)S(1)}, bf16[256,256]{1,0:T(8,128)(2,1)}, u32[]{:S(2)}) copy-start(bf16[256,256]{1,0:T(8,128)(2,1)} %wo.3) | copy-start | bytes 393220
  10.2 7.4 %copy-start.6 = (f32[3,256]{1,0:T(4,128)S(1)}, f32[3,256]{1,0:T(4,128)}, u32[]{:S(2)}) copy-start(f32[3,256]{1,0:T(4,128)} %bias.3) | copy-start | bytes 9220
  11.2 17.4 %collective-permute-start.3 = (bf16[23,5,8,256]{3,2,1,0:T(8,128)(2,1)S(1)}, bf16[23,5,8,256]{3,2,1,0:T(8,128)(2,1)S(1)}, u32[]{:S(2)}, u32[]{:S(2)}) collective-permute-start(bf16[23,5,8,256]{3,2,1,0:T(8,128)(2,1)S(1)} %get-tuple-element.29), channel_id=1, source_target_pairs={{0,1},{1,2},{2,3},{3,4},{4,5},{5,6},{6,7},{7,8},{8,9},{9,10},{10,1... | collective-permute-start | bytes 1413128 | tf_op jit(solution)/shard_map/ppermute | solution.py:426
  15.6 16.7 %collective-permute-start.4 = (bf16[23,5,8,256]{3,2,1,0:T(8,128)(2,1)S(1)}, bf16[23,5,8,256]{3,2,1,0:T(8,128)(2,1)S(1)}, u32[]{:S(2)}, u32[]{:S(2)}) collective-permute-start(bf16[23,5,8,256]{3,2,1,0:T(8,128)(2,1)S(1)} %get-tuple-element.30), channel_id=1, source_target_pairs={{1,0},{2,1},{3,2},{4,3},{5,4},{6,5},{7,6},{8,7},{9,8},{10,9},{11,1... | collective-permute-start | bytes 1413128 | tf_op jit(solution)/shard_map/ppermute | solution.py:425
  48.6 3.0 %collective-permute-start.5 = (bf16[4,17,8,256]{3,2,1,0:T(8,128)(2,1)S(1)}, bf16[4,17,8,256]{3,2,1,0:T(8,128)(2,1)S(1)}, u32[]{:S(2)}, u32[]{:S(2)}) collective-permute-start(bf16[4,17,8,256]{3,2,1,0:T(8,128)(2,1)S(1)} %get-tuple-element.40), channel_id=1, source_target_pairs={{0,128},{128,0},{1,129},{129,1},{2,130},{130,2},{3,131},{131,3},{4... | collective-permute-start | bytes 835592 | tf_op jit(solution)/shard_map/ppermute | solution.py:462

commit v3 on v2

--- a/solution.py
+++ b/solution.py
@@ -91,21 +91,21 @@
             ht[e, col] = old.astype(BF)
             past.append(old)
             if col < 3:
-                left[e, col] = lat.astype(BF)
+                left[e * 4 + col] = lat.astype(BF)
             if col >= 5:
-                right[e, col - 5] = lat.astype(BF)
-        left[e, 3] = jnp.where(sub < 6, past[0], pltpu.roll(past[2], 6, 0)).astype(BF)
-        left[e, 4] = past[1].astype(BF)
-        right[e, 3] = jnp.where(sub < 6, past[7], pltpu.roll(past[5], 6, 0)).astype(BF)
-        right[e, 4] = past[6].astype(BF)
+                right[e * 4 + col - 5] = lat.astype(BF)
+        left[e * 4 + 3] = jnp.where(sub < 6, past[0], pltpu.roll(past[2], 6, 0)).astype(BF)
+        right[e * 4 + 3] = jnp.where(sub < 6, past[7], pltpu.roll(past[5], 6, 0)).astype(BF)
+        return past[1], past[6]
 
     def pair(i, carry):
-        row(2 * i, 0)
-        row(2 * i + 1, 1)
+        for dst, low, high in zip((left, right), row(2 * i, 0), row(2 * i + 1, 1)):
+            dst[EXT * 4 + i] = jnp.where(sub < 4, low, pltpu.roll(high, 4, 0)).astype(BF)
         return carry
 
     lax.fori_loop(0, EXT // 2, pair, 0)
-    row(EXT - 1, 0)
+    for dst, low in zip((left, right), row(EXT - 1, 0)):
+        dst[EXT * 4 + EXT // 2] = low.astype(BF)
 
 
 def put(dst, r, at, now, past, layer):
@@ -167,8 +167,13 @@
     dst[0:tiles, 1, 0:count] = odd.reshape(tiles, count, T, C)
 
 
+def far_past(side, r):
+    v = side[EXT * 4 + r // 2].astype(F32)
+    return jnp.where(r % 2 == 0, v, pltpu.roll(v, 4, 0))
+
+
 def silu(v):
-    return v / (1.0 + jnp.exp(-v))
+    return 0.5 * v * (1.0 + jnp.tanh(0.5 * v))
 
 
 def row_limits(border):
@@ -293,12 +298,12 @@
 
     def fill(r, carry):
         for side, at in ((from_left, 0), (from_right, 11)):
-            t1 = side[r, 3].astype(F32)
-            t2 = side[r, 4].astype(F32)
+            t1 = side[r * 4 + 3].astype(F32)
+            t2 = far_past(side, r)
             t3 = pltpu.roll(t1, 2, 0)
             order = (t3, t2, t1) if at == 0 else (t1, t2, t3)
             past = jnp.concatenate([v[None] for v in order], 0)
-            put(x, r, at, side[r, 0:3].astype(F32), past, 0)
+            put(x, r, at, side[pl.ds(r * 4, 3)].astype(F32), past, 0)
         return carry
 
     lax.fori_loop(0, EXT, fill, 0, unroll=2)
@@ -311,12 +316,12 @@
         e = r + 1
         put(y, r, 0, jnp.concatenate(
             [jnp.where(ok & has_left, v[0:2], 0.0), jnp.where(ok, v[2:3], 0.0)], 0),
-            jnp.concatenate([from_left[e, 4:5].astype(F32), from_left[e, 3:4].astype(F32),
+            jnp.concatenate([far_past(from_left, e)[None], from_left[e * 4 + 3].astype(F32)[None],
                              ht[e, 0:1].astype(F32)], 0), 1)
         put(y, r, 9, jnp.concatenate(
             [jnp.where(ok, v[3:4], 0.0), jnp.where(ok & has_right, v[4:6], 0.0)], 0),
-            jnp.concatenate([ht[e, 7:8].astype(F32), from_right[e, 3:4].astype(F32),
-                             from_right[e, 4:5].astype(F32)], 0), 1)
+            jnp.concatenate([ht[e, 7:8].astype(F32), from_right[e * 4 + 3].astype(F32)[None],
+                             far_past(from_right, e)[None]], 0), 1)
         return carry
 
     lax.fori_loop(0, 21, one, 0, unroll=3)
@@ -329,10 +334,10 @@
         e = r + 2
         put(z, r, 0, jnp.concatenate(
             [jnp.where(ok & has_left, v[0:1], 0.0), jnp.where(ok, v[1:3], 0.0)], 0),
-            jnp.concatenate([from_left[e, 3:4].astype(F32), ht[e, 0:2].astype(F32)], 0), 2)
+            jnp.concatenate([from_left[e * 4 + 3].astype(F32)[None], ht[e, 0:2].astype(F32)], 0), 2)
         put(z, r, 7, jnp.concatenate(
             [jnp.where(ok, v[3:5], 0.0), jnp.where(ok & has_right, v[5:6], 0.0)], 0),
-            jnp.concatenate([ht[e, 6:8].astype(F32), from_right[e, 3:4].astype(F32)], 0), 2)
+            jnp.concatenate([ht[e, 6:8].astype(F32), from_right[e * 4 + 3].astype(F32)[None]], 0), 2)
         return carry
 
     lax.fori_loop(0, 19, two, 0, unroll=2)
@@ -340,7 +345,7 @@
     cols = (0, 1, 2, 5, 6, 7)
     own = jnp.concatenate([lt[3:20, 0:3], lt[3:20, 5:8]], 1).astype(F32)
     hidden = (res[0:9].reshape(18, 6, T, C)[0:17] + own).astype(BF).astype(F32)
-    done = attend_all(hidden.reshape(HALF * 6 * T, C), cols, 3, wq, wk, wv, wo, keys, values,
+    done = attend_all(hidden.reshape(HALF * 6 * T, C), cols, 6, wq, wk, wv, wo, keys, values,
                       qs, ks, vs, mix).reshape(HALF, 6, T, C)
     done = jnp.concatenate([done[:, 0:3], inner[...].astype(F32), done[:, 3:6]], 1)
     done = done.reshape(HALF * COLS * T, C)
@@ -356,7 +361,7 @@
                 dst[f, r] = v.astype(BF)
         return carry
 
-    lax.fori_loop(0, HALF, turn, 0)
+    lax.fori_loop(0, HALF, turn, 0, unroll=2)
 
 
 def merge(mine, got, out, sems):
@@ -407,7 +412,7 @@
     )(weights)
 
     tiles = shape(EXT, COLS, T, C)
-    side = shape(EXT, 5, T, C)
+    side = shape(EXT * 4 + (EXT + 1) // 2, T, C)
     lt, ht, left, right, held = pl.pallas_call(
         assemble,
         out_shape=(tiles, tiles, side, side, shape(3 * LAYER_K, C)),

time: 52.8 us -> 50.7 us (0.960)
  Pallas kernels: 32.3 us -> 30.7 us
    pallas_call x1, Pallas kernels: 16.2 us -> 15.2 us  [local(): pl.pallas_call(exterior, out_shape=(shape(4, HALF, COLS, C), shape(4, HAL...]
    pallas_call x1, Pallas kernels: 11 us -> 10.5 us  [local(): pl.pallas_call(interior, out_shape=(shape(17, 2, T, C), shape(3 * LAYER_K...]
where the time goes in v3:
time: 50.7 us; the launch traced here: 50.5 us
  Pallas kernels  30.7 us (61%)
  starting transfers between devices  14.9 us (29%)
  waiting for transfers between devices  4.42 us (9%)
    pallas_call x1, Pallas kernels, local(): pl.pallas_call(exterior, out_shape=(shape(4, HALF, COLS, C), shape(4, HAL...  15.2 us
    pallas_call x1, Pallas kernels, local(): pl.pallas_call(interior, out_shape=(shape(17, 2, T, C), shape(3 * LAYER_K...  10.5 us
    ppermute x1, starting transfers between devices, local(): lax.ppermute(right, 'col', [(i, i + 1) for i in range(n_col - 1)])  4.42 us
    ppermute x1, starting transfers between devices, local(): halo_b = lax.ppermute(msg_b, ('tm', 'row'), pairs_b)  3.95 us
    ppermute x1, waiting for transfers between devices, local(): lax.ppermute(left, 'col', [(i + 1, i) for i in range(n_col - 1)])  3.22 us
    ppermute x1, starting transfers between devices, local(): halo_a = lax.ppermute(msg_a, ('tm', 'row'), pairs_a)  2.16 us
    pallas_call x1, Pallas kernels, local(): pl.pallas_call(load_first, out_shape=shape(3 * LAYER_K, C), in_specs=[ANY...  2.01 us
    ppermute x1, starting transfers between devices, local(): lax.ppermute(left, 'col', [(i + 1, i) for i in range(n_col - 1)])  1.92 us
  transfers between devices with their start and end apart: 6, of which 2 were waited for; matrix products, arithmetic and copies ran while one was open for 0% of the time, Pallas kernels for 27%

profile of v3, /device:TPU:123, one launch (start us, length us, event | category | flops | bytes accessed | tf_op | source)
XLA Modules:
  0.0 50.5 jit_solution(4640995263229138935)
XLA Ops:
  0.0 0.7 %collective-permute-start = (bf16[4,34,8,256]{3,2,1,0:T(8,128)(2,1)}, bf16[4,34,8,256]{3,2,1,0:T(8,128)(2,1)S(1)}, u32[]{:S(2)}, u32[]{:S(2)}) collective-permute-start(bf16[4,34,8,256]{3,2,1,0:T(8,128)(2,1)} %latent.1), channel_id=1, source_target_pairs={{0,128},{128,0},{1,129},{129,1},{2,130},{130,2},{3,131},{131,3},{4... | collective-permute-start | bytes 1671176 | tf_op jit(solution)/shard_map/ppermute | solution.py:395
  0.7 1.3 %pack_rows.1 = (bf16[10,3,8,256]{3,2,1,0:T(8,128)(2,1)S(1)}, bf16[4,3,8,256]{3,2,1,0:T(8,128)(2,1)S(1)}, bf16[4,20,8,256]{3,2,1,0:T(8,128)(2,1)S(1)}, bf16[6,20,8,256]{3,2,1,0:T(8,128)(2,1)S(1)}) custom-call(bf16[4,34,8,256]{3,2,1,0:T(8,128)(2,1)} %latent.1, bf16[6,34,8,256]{3,2,1,0:T(8,128)(2,1)} %bitcast.4), custom_call_target="tpu_custom_call" | custom-call | tf_op jit(solution)/shard_map/pack_rows/pallas_call | solution.py:385
  2.0 2.2 %collective-permute-start.1 = (bf16[10,3,8,256]{3,2,1,0:T(8,128)(2,1)S(1)}, bf16[10,3,8,256]{3,2,1,0:T(8,128)(2,1)S(1)}, u32[]{:S(2)}, u32[]{:S(2)}) collective-permute-start(bf16[10,3,8,256]{3,2,1,0:T(8,128)(2,1)S(1)} %get-tuple-element.25), channel_id=1, source_target_pairs={{0,32},{32,64},{64,96},{160,128},{192,160},{224,192},{1,33},{33,65... | collective-permute-start | bytes 368648 | tf_op jit(solution)/shard_map/ppermute | solution.py:400
  4.1 4.0 %collective-permute-start.2 = (bf16[4,3,8,256]{3,2,1,0:T(8,128)(2,1)S(1)}, bf16[4,3,8,256]{3,2,1,0:T(8,128)(2,1)S(1)}, u32[]{:S(2)}, u32[]{:S(2)}) collective-permute-start(bf16[4,3,8,256]{3,2,1,0:T(8,128)(2,1)S(1)} %get-tuple-element.26), channel_id=1, source_target_pairs={{128,32},{160,64},{192,96},{32,128},{64,160},{96,192},{129,33},{16... | collective-permute-start | bytes 147464 | tf_op jit(solution)/shard_map/ppermute | solution.py:401
  8.1 2.0 %load_weights.1.held = bf16[20736,256]{1,0:T(8,128)(2,1)S(1)} custom-call(bf16[20736,256]{1,0:T(8,128)(2,1)} %bitcast.2), custom_call_target="tpu_custom_call" | custom-call | bytes 4194304 | tf_op jit(solution)/shard_map/load_weights/pallas_call | solution.py:403
  10.1 0.0 copy-start
  10.1 0.0 copy-start.1
  10.1 0.0 copy-start.2
  10.1 0.0 copy-start.3
  10.2 0.0 copy-start.4
  10.2 0.0 copy-start.5
  10.2 0.0 copy-start.6
  10.2 0.0 collective-permute-done.2.halo_b
  10.2 0.0 collective-permute-done.1.halo_a
  10.2 0.0 collective-permute-done.other
  10.2 1.0 %assemble.1 = (bf16[23,8,8,256]{3,2,1,0:T(8,128)(2,1)S(1)}, bf16[23,8,8,256]{3,2,1,0:T(8,128)(2,1)S(1)}, bf16[104,8,256]{2,1,0:T(8,128)(2,1)S(1)}, bf16[104,8,25...) custom-call(bf16[4,20,8,256]{3,2,1,0:T(8,128)(2,1)S(1)} %get-tuple-element.23.own, ...), custom_call_target="tpu_custom_call", output_to_operand_aliasing={{4}: (5, {})} | custom-call | tf_op jit(solution)/shard_map/assemble/pallas_call | solution.py:416
  11.2 4.4 %collective-permute-start.3 = (bf16[104,8,256]{2,1,0:T(8,128)(2,1)S(1)}, bf16[104,8,256]{2,1,0:T(8,128)(2,1)S(1)}, u32[]{:S(2)}, u32[]{:S(2)}) collective-permute-start(bf16[104,8,256]{2,1,0:T(8,128)(2,1)S(1)} %get-tuple-element.29), channel_id=1, source_target_pairs={{0,1},{1,2},{2,3},{3,4},{4,5},{5,6},{6,7},{7,8},{8,9},{9,10},{10,1... | collective-permute-start | bytes 1277960 | tf_op jit(solution)/shard_map/ppermute | solution.py:431
  15.6 1.9 %collective-permute-start.4 = (bf16[104,8,256]{2,1,0:T(8,128)(2,1)S(1)}, bf16[104,8,256]{2,1,0:T(8,128)(2,1)S(1)}, u32[]{:S(2)}, u32[]{:S(2)}) collective-permute-start(bf16[104,8,256]{2,1,0:T(8,128)(2,1)S(1)} %get-tuple-element.30), channel_id=1, source_target_pairs={{1,0},{2,1},{3,2},{4,3},{5,4},{6,5},{7,6},{8,7},{9,8},{10,9},{11,1... | collective-permute-start | bytes 1277960 | tf_op jit(solution)/shard_map/ppermute | solution.py:430
  17.6 0.0 copy-done
  17.6 0.0 copy-done.1
  17.6 0.0 copy-done.2
  17.6 0.0 copy-done.3
  17.6 0.0 copy-done.4
  17.6 0.0 copy-done.5
  17.6 0.0 copy-done.6
  17.6 10.5 %interior.1 = (bf16[17,2,8,256]{3,2,1,0:T(8,128)(2,1)S(1)}, bf16[20736,256]{1,0:T(8,128)(2,1)S(1)}, f32[3,12,2,14,8,256]{5,4,3,2,1,0:T(8,128)S(1)}, f32[3,11,2,1...) custom-call(bf16[23,8,8,256]{3,2,1,0:T(8,128)(2,1)S(1)} %get-tuple-e, ...), custom_call_target="tpu_custom_call", output_to_operand_aliasing={{1}: (2, {})} | custom-call | flops 6681526272 | bytes 14680064 | tf_op jit(solution)/shard_map/interior/pallas_call | solution.py:436
  28.1 0.0 collective-permute-done.3.from_left
  28.1 3.2 %collective-permute-done.4.from_right = bf16[104,8,256]{2,1,0:T(8,128)(2,1)S(1)} collective-permute-done((bf16[104,8,256]{2,1,0:T(8,128)(2,1)S(1)}, bf16[104,8,256]{2,1,0:T(8,128)(2,1)S(1)}, u32[]{:S(2)}, u32[]{:S(2)}) %collective-permute-start.4) | collective-permute-done | bytes 426016 | tf_op jit(solution)/shard_map/ppermute | solution.py:430
  31.4 15.2 %exterior.1 = (bf16[4,17,8,256]{3,2,1,0:T(8,128)(2,1)S(1)}, bf16[4,17,8,256]{3,2,1,0:T(8,128)(2,1)S(1)}, f32[3,12,2,14,8,256]{5,4,3,2,1,0:T(8,128)S(1)}, f32[3,1...) custom-call(bf16[23,8,8,256]{3,2,1,0:T(8,128)(2,1)S(1)} %get-tuple-e, ...), custom_call_target="tpu_custom_call", output_to_operand_aliasing={{2}: (11, {}), {3}: (12, {}), {4}: (13, {})} | custom-call | flops 10616832000 | bytes 18874368 | tf_op jit(solution)/shard_map/exterior/pallas_call | solution.py:452
  46.5 1.8 %collective-permute-start.5 = (bf16[4,17,8,256]{3,2,1,0:T(8,128)(2,1)S(1)}, bf16[4,17,8,256]{3,2,1,0:T(8,128)(2,1)S(1)}, u32[]{:S(2)}, u32[]{:S(2)}) collective-permute-start(bf16[4,17,8,256]{3,2,1,0:T(8,128)(2,1)S(1)} %get-tuple-element.40), channel_id=1, source_target_pairs={{0,128},{128,0},{1,129},{129,1},{2,130},{130,2},{3,131},{131,3},{4... | collective-permute-start | bytes 835592 | tf_op jit(solution)/shard_map/ppermute | solution.py:467
  48.3 1.2 %collective-permute-done.5.got = bf16[4,17,8,256]{3,2,1,0:T(8,128)(2,1)S(1)} collective-permute-done((bf16[4,17,8,256]{3,2,1,0:T(8,128)(2,1)S(1)}, bf16[4,17,8,256]{3,2,1,0:T(8,128)(2,1)S(1)}, u32[]{:S(2)}, u32[]{:S(2)}) %collective-permute-start.5) | collective-permute-done | bytes 278560 | tf_op jit(solution)/shard_map/ppermute | solution.py:467
  49.5 0.8 %merge.1 = bf16[4,34,8,256]{3,2,1,0:T(8,128)(2,1)} custom-call(bf16[4,17,8,256]{3,2,1,0:T(8,128)(2,1)S(1)} %get-tuple-element.39.mine, bf16[4,17,8,256]{3,2,1,0:T(8,128)(2,1)S(1)} %collective-permute-done.5.got), custom_call_target="tpu_custom_call" | custom-call | tf_op jit(solution)/shard_map/merge/pallas_call | solution.py:468
Async XLA Ops:
  0.0 10.2 %collective-permute-start = (bf16[4,34,8,256]{3,2,1,0:T(8,128)(2,1)}, bf16[4,34,8,256]{3,2,1,0:T(8,128)(2,1)S(1)}, u32[]{:S(2)}, u32[]{:S(2)}) collective-permute-start(bf16[4,34,8,256]{3,2,1,0:T(8,128)(2,1)} %latent.1), channel_id=1, source_target_pairs={{0,128},{128,0},{1,129},{129,1},{2,130},{130,2},{3,131},{131,3},{4... | collective-permute-start | bytes 1671176 | tf_op jit(solution)/shard_map/ppermute | solution.py:395
  2.0 8.2 %collective-permute-start.1 = (bf16[10,3,8,256]{3,2,1,0:T(8,128)(2,1)S(1)}, bf16[10,3,8,256]{3,2,1,0:T(8,128)(2,1)S(1)}, u32[]{:S(2)}, u32[]{:S(2)}) collective-permute-start(bf16[10,3,8,256]{3,2,1,0:T(8,128)(2,1)S(1)} %get-tuple-element.25), channel_id=1, source_target_pairs={{0,32},{32,64},{64,96},{160,128},{192,160},{224,192},{1,33},{33,65... | collective-permute-start | bytes 368648 | tf_op jit(solution)/shard_map/ppermute | solution.py:400
  4.1 6.1 %collective-permute-start.2 = (bf16[4,3,8,256]{3,2,1,0:T(8,128)(2,1)S(1)}, bf16[4,3,8,256]{3,2,1,0:T(8,128)(2,1)S(1)}, u32[]{:S(2)}, u32[]{:S(2)}) collective-permute-start(bf16[4,3,8,256]{3,2,1,0:T(8,128)(2,1)S(1)} %get-tuple-element.26), channel_id=1, source_target_pairs={{128,32},{160,64},{192,96},{32,128},{64,160},{96,192},{129,33},{16... | collective-permute-start | bytes 147464 | tf_op jit(solution)/shard_map/ppermute | solution.py:401
  10.1 7.5 %copy-start = (bf16[2,34,8,256]{3,2,1,0:T(8,128)(2,1)S(1)}, bf16[2,34,8,256]{3,2,1,0:T(8,128)(2,1)}, u32[]{:S(2)}) copy-start(bf16[2,34,8,256]{3,2,1,0:T(8,128)(2,1)} %key_cache.1) | copy-start | bytes 835588
  10.1 7.4 %copy-start.1 = (bf16[2,34,8,256]{3,2,1,0:T(8,128)(2,1)S(1)}, bf16[2,34,8,256]{3,2,1,0:T(8,128)(2,1)}, u32[]{:S(2)}) copy-start(bf16[2,34,8,256]{3,2,1,0:T(8,128)(2,1)} %value_cache.1) | copy-start | bytes 835588
  10.1 7.4 %copy-start.2 = (bf16[256,256]{1,0:T(8,128)(2,1)S(1)}, bf16[256,256]{1,0:T(8,128)(2,1)}, u32[]{:S(2)}) copy-start(bf16[256,256]{1,0:T(8,128)(2,1)} %wq.3) | copy-start | bytes 393220
  10.1 7.4 %copy-start.3 = (bf16[256,256]{1,0:T(8,128)(2,1)S(1)}, bf16[256,256]{1,0:T(8,128)(2,1)}, u32[]{:S(2)}) copy-start(bf16[256,256]{1,0:T(8,128)(2,1)} %wk.3) | copy-start | bytes 393220
  10.2 7.4 %copy-start.4 = (bf16[256,256]{1,0:T(8,128)(2,1)S(1)}, bf16[256,256]{1,0:T(8,128)(2,1)}, u32[]{:S(2)}) copy-start(bf16[256,256]{1,0:T(8,128)(2,1)} %wv.3) | copy-start | bytes 393220
  10.2 7.4 %copy-start.5 = (bf16[256,256]{1,0:T(8,128)(2,1)S(1)}, bf16[256,256]{1,0:T(8,128)(2,1)}, u32[]{:S(2)}) copy-start(bf16[256,256]{1,0:T(8,128)(2,1)} %wo.3) | copy-start | bytes 393220
  10.2 7.4 %copy-start.6 = (f32[3,256]{1,0:T(4,128)S(1)}, f32[3,256]{1,0:T(4,128)}, u32[]{:S(2)}) copy-start(f32[3,256]{1,0:T(4,128)} %bias.3) | copy-start | bytes 9220
  11.2 16.9 %collective-permute-start.3 = (bf16[104,8,256]{2,1,0:T(8,128)(2,1)S(1)}, bf16[104,8,256]{2,1,0:T(8,128)(2,1)S(1)}, u32[]{:S(2)}, u32[]{:S(2)}) collective-permute-start(bf16[104,8,256]{2,1,0:T(8,128)(2,1)S(1)} %get-tuple-element.29), channel_id=1, source_target_pairs={{0,1},{1,2},{2,3},{3,4},{4,5},{5,6},{6,7},{7,8},{8,9},{9,10},{10,1... | collective-permute-start | bytes 1277960 | tf_op jit(solution)/shard_map/ppermute | solution.py:431
  15.6 15.7 %collective-permute-start.4 = (bf16[104,8,256]{2,1,0:T(8,128)(2,1)S(1)}, bf16[104,8,256]{2,1,0:T(8,128)(2,1)S(1)}, u32[]{:S(2)}, u32[]{:S(2)}) collective-permute-start(bf16[104,8,256]{2,1,0:T(8,128)(2,1)S(1)} %get-tuple-element.30), channel_id=1, source_target_pairs={{1,0},{2,1},{3,2},{4,3},{5,4},{6,5},{7,6},{8,7},{9,8},{10,9},{11,1... | collective-permute-start | bytes 1277960 | tf_op jit(solution)/shard_map/ppermute | solution.py:430
  46.5 3.0 %collective-permute-start.5 = (bf16[4,17,8,256]{3,2,1,0:T(8,128)(2,1)S(1)}, bf16[4,17,8,256]{3,2,1,0:T(8,128)(2,1)S(1)}, u32[]{:S(2)}, u32[]{:S(2)}) collective-permute-start(bf16[4,17,8,256]{3,2,1,0:T(8,128)(2,1)S(1)} %get-tuple-element.40), channel_id=1, source_target_pairs={{0,128},{128,0},{1,129},{129,1},{2,130},{130,2},{3,131},{131,3},{4... | collective-permute-start | bytes 835592 | tf_op jit(solution)/shard_map/ppermute | solution.py:467

commit v4 on v3

--- a/solution.py
+++ b/solution.py
@@ -283,7 +283,7 @@
     for src, dst in ((ck, keys), (cv, values)):
         dst[:, 0:HALF] = src[...].astype(F32)
         dst[:, HALF:] = jnp.zeros((2, 1, COLS, C), F32)
-    done = attend_all(hidden.reshape(HALF * 2 * T, C), (3, 4), 9, wq, wk, wv, wo, keys, values,
+    done = attend_all(hidden.reshape(HALF * 2 * T, C), (3, 4), 18, wq, wk, wv, wo, keys, values,
                       qs, ks, vs, mix)
     out[...] = done.reshape(HALF, 2, T, C).astype(BF)
 
@@ -345,7 +345,7 @@
     cols = (0, 1, 2, 5, 6, 7)
     own = jnp.concatenate([lt[3:20, 0:3], lt[3:20, 5:8]], 1).astype(F32)
     hidden = (res[0:9].reshape(18, 6, T, C)[0:17] + own).astype(BF).astype(F32)
-    done = attend_all(hidden.reshape(HALF * 6 * T, C), cols, 6, wq, wk, wv, wo, keys, values,
+    done = attend_all(hidden.reshape(HALF * 6 * T, C), cols, 9, wq, wk, wv, wo, keys, values,
                       qs, ks, vs, mix).reshape(HALF, 6, T, C)
     done = jnp.concatenate([done[:, 0:3], inner[...].astype(F32), done[:, 3:6]], 1)
     done = done.reshape(HALF * COLS * T, C)
@@ -361,7 +361,7 @@
                 dst[f, r] = v.astype(BF)
         return carry
 
-    lax.fori_loop(0, HALF, turn, 0, unroll=2)
+    lax.fori_loop(0, HALF, turn, 0, unroll=4)
 
 
 def merge(mine, got, out, sems):

time: 50.7 us -> 50.7 us (level)
  Pallas kernels: 30.7 us -> 30 us
  waiting for transfers between devices: 4.42 us -> 5.08 us
    ppermute x1, waiting for transfers between devices: 3.22 us -> 3.89 us  [local(): lax.ppermute(left, 'col', [(i + 1, i) for i in range(n_col - 1)])]
    pallas_call x1, Pallas kernels: 10.5 us -> 9.82 us  [local(): pl.pallas_call(interior, out_shape=(shape(17, 2, T, C), shape(3 * LAYER_K...]
  transfers between devices with their start and end apart: 6 -> 6, of which waited for: 2 -> 2; matrix products, arithmetic and copies ran while one was open for 0% -> 0% of each run, Pallas kernels for 27% -> 26%
where the time goes in v4:
time: 50.7 us; the launch traced here: 50.4 us
  Pallas kernels  30 us (59%)
  starting transfers between devices  14.9 us (29%)
  waiting for transfers between devices  5.08 us (10%)
    pallas_call x1, Pallas kernels, local(): pl.pallas_call(exterior, out_shape=(shape(4, HALF, COLS, C), shape(4, HAL...  15.1 us
    pallas_call x1, Pallas kernels, local(): pl.pallas_call(interior, out_shape=(shape(17, 2, T, C), shape(3 * LAYER_K...  9.82 us
    ppermute x1, starting transfers between devices, local(): lax.ppermute(right, 'col', [(i, i + 1) for i in range(n_col - 1)])  4.42 us
    ppermute x1, starting transfers between devices, local(): halo_b = lax.ppermute(msg_b, ('tm', 'row'), pairs_b)  3.95 us
    ppermute x1, waiting for transfers between devices, local(): lax.ppermute(left, 'col', [(i + 1, i) for i in range(n_col - 1)])  3.89 us
    ppermute x1, starting transfers between devices, local(): halo_a = lax.ppermute(msg_a, ('tm', 'row'), pairs_a)  2.16 us
    pallas_call x1, Pallas kernels, local(): pl.pallas_call(load_first, out_shape=shape(3 * LAYER_K, C), in_specs=[ANY...  2.01 us
    ppermute x1, starting transfers between devices, local(): lax.ppermute(left, 'col', [(i + 1, i) for i in range(n_col - 1)])  1.92 us
  transfers between devices with their start and end apart: 6, of which 2 were waited for; matrix products, arithmetic and copies ran while one was open for 0% of the time, Pallas kernels for 26%

profile of v4, /device:TPU:123, one launch (start us, length us, event | category | flops | bytes accessed | tf_op | source)
XLA Modules:
  0.0 50.4 jit_solution(6602652679415768529)
XLA Ops:
  0.0 0.7 %collective-permute-start = (bf16[4,34,8,256]{3,2,1,0:T(8,128)(2,1)}, bf16[4,34,8,256]{3,2,1,0:T(8,128)(2,1)S(1)}, u32[]{:S(2)}, u32[]{:S(2)}) collective-permute-start(bf16[4,34,8,256]{3,2,1,0:T(8,128)(2,1)} %latent.1), channel_id=1, source_target_pairs={{0,128},{128,0},{1,129},{129,1},{2,130},{130,2},{3,131},{131,3},{4... | collective-permute-start | bytes 1671176 | tf_op jit(solution)/shard_map/ppermute | solution.py:395
  0.7 1.3 %pack_rows.1 = (bf16[10,3,8,256]{3,2,1,0:T(8,128)(2,1)S(1)}, bf16[4,3,8,256]{3,2,1,0:T(8,128)(2,1)S(1)}, bf16[4,20,8,256]{3,2,1,0:T(8,128)(2,1)S(1)}, bf16[6,20,8,256]{3,2,1,0:T(8,128)(2,1)S(1)}) custom-call(bf16[4,34,8,256]{3,2,1,0:T(8,128)(2,1)} %latent.1, bf16[6,34,8,256]{3,2,1,0:T(8,128)(2,1)} %bitcast.4), custom_call_target="tpu_custom_call" | custom-call | tf_op jit(solution)/shard_map/pack_rows/pallas_call | solution.py:385
  2.0 2.2 %collective-permute-start.1 = (bf16[10,3,8,256]{3,2,1,0:T(8,128)(2,1)S(1)}, bf16[10,3,8,256]{3,2,1,0:T(8,128)(2,1)S(1)}, u32[]{:S(2)}, u32[]{:S(2)}) collective-permute-start(bf16[10,3,8,256]{3,2,1,0:T(8,128)(2,1)S(1)} %get-tuple-element.25), channel_id=1, source_target_pairs={{0,32},{32,64},{64,96},{160,128},{192,160},{224,192},{1,33},{33,65... | collective-permute-start | bytes 368648 | tf_op jit(solution)/shard_map/ppermute | solution.py:400
  4.1 4.0 %collective-permute-start.2 = (bf16[4,3,8,256]{3,2,1,0:T(8,128)(2,1)S(1)}, bf16[4,3,8,256]{3,2,1,0:T(8,128)(2,1)S(1)}, u32[]{:S(2)}, u32[]{:S(2)}) collective-permute-start(bf16[4,3,8,256]{3,2,1,0:T(8,128)(2,1)S(1)} %get-tuple-element.26), channel_id=1, source_target_pairs={{128,32},{160,64},{192,96},{32,128},{64,160},{96,192},{129,33},{16... | collective-permute-start | bytes 147464 | tf_op jit(solution)/shard_map/ppermute | solution.py:401
  8.1 2.0 %load_weights.1.held = bf16[20736,256]{1,0:T(8,128)(2,1)S(1)} custom-call(bf16[20736,256]{1,0:T(8,128)(2,1)} %bitcast.2), custom_call_target="tpu_custom_call" | custom-call | bytes 4194304 | tf_op jit(solution)/shard_map/load_weights/pallas_call | solution.py:403
  10.1 0.0 copy-start
  10.1 0.0 copy-start.1
  10.1 0.0 copy-start.2
  10.1 0.0 copy-start.3
  10.2 0.0 copy-start.4
  10.2 0.0 copy-start.5
  10.2 0.0 copy-start.6
  10.2 0.0 collective-permute-done.2.halo_b
  10.2 0.0 collective-permute-done.1.halo_a
  10.2 0.0 collective-permute-done.other
  10.2 1.0 %assemble.1 = (bf16[23,8,8,256]{3,2,1,0:T(8,128)(2,1)S(1)}, bf16[23,8,8,256]{3,2,1,0:T(8,128)(2,1)S(1)}, bf16[104,8,256]{2,1,0:T(8,128)(2,1)S(1)}, bf16[104,8,25...) custom-call(bf16[4,20,8,256]{3,2,1,0:T(8,128)(2,1)S(1)} %get-tuple-element.23.own, ...), custom_call_target="tpu_custom_call", output_to_operand_aliasing={{4}: (5, {})} | custom-call | tf_op jit(solution)/shard_map/assemble/pallas_call | solution.py:416
  11.2 4.4 %collective-permute-start.3 = (bf16[104,8,256]{2,1,0:T(8,128)(2,1)S(1)}, bf16[104,8,256]{2,1,0:T(8,128)(2,1)S(1)}, u32[]{:S(2)}, u32[]{:S(2)}) collective-permute-start(bf16[104,8,256]{2,1,0:T(8,128)(2,1)S(1)} %get-tuple-element.29), channel_id=1, source_target_pairs={{0,1},{1,2},{2,3},{3,4},{4,5},{5,6},{6,7},{7,8},{8,9},{9,10},{10,1... | collective-permute-start | bytes 1277960 | tf_op jit(solution)/shard_map/ppermute | solution.py:431
  15.6 1.9 %collective-permute-start.4 = (bf16[104,8,256]{2,1,0:T(8,128)(2,1)S(1)}, bf16[104,8,256]{2,1,0:T(8,128)(2,1)S(1)}, u32[]{:S(2)}, u32[]{:S(2)}) collective-permute-start(bf16[104,8,256]{2,1,0:T(8,128)(2,1)S(1)} %get-tuple-element.30), channel_id=1, source_target_pairs={{1,0},{2,1},{3,2},{4,3},{5,4},{6,5},{7,6},{8,7},{9,8},{10,9},{11,1... | collective-permute-start | bytes 1277960 | tf_op jit(solution)/shard_map/ppermute | solution.py:430
  17.6 0.0 copy-done
  17.6 0.0 copy-done.1
  17.6 0.0 copy-done.2
  17.6 0.0 copy-done.3
  17.6 0.0 copy-done.4
  17.6 0.0 copy-done.5
  17.6 0.0 copy-done.6
  17.6 9.8 %interior.1 = (bf16[17,2,8,256]{3,2,1,0:T(8,128)(2,1)S(1)}, bf16[20736,256]{1,0:T(8,128)(2,1)S(1)}, f32[3,12,2,14,8,256]{5,4,3,2,1,0:T(8,128)S(1)}, f32[3,11,2,1...) custom-call(bf16[23,8,8,256]{3,2,1,0:T(8,128)(2,1)S(1)} %get-tuple-e, ...), custom_call_target="tpu_custom_call", output_to_operand_aliasing={{1}: (2, {})} | custom-call | flops 6681526272 | bytes 14680064 | tf_op jit(solution)/shard_map/interior/pallas_call | solution.py:436
  27.5 0.0 collective-permute-done.3.from_left
  27.5 3.9 %collective-permute-done.4.from_right = bf16[104,8,256]{2,1,0:T(8,128)(2,1)S(1)} collective-permute-done((bf16[104,8,256]{2,1,0:T(8,128)(2,1)S(1)}, bf16[104,8,256]{2,1,0:T(8,128)(2,1)S(1)}, u32[]{:S(2)}, u32[]{:S(2)}) %collective-permute-start.4) | collective-permute-done | bytes 426016 | tf_op jit(solution)/shard_map/ppermute | solution.py:430
  31.4 15.1 %exterior.1 = (bf16[4,17,8,256]{3,2,1,0:T(8,128)(2,1)S(1)}, bf16[4,17,8,256]{3,2,1,0:T(8,128)(2,1)S(1)}, f32[3,12,2,14,8,256]{5,4,3,2,1,0:T(8,128)S(1)}, f32[3,1...) custom-call(bf16[23,8,8,256]{3,2,1,0:T(8,128)(2,1)S(1)} %get-tuple-e, ...), custom_call_target="tpu_custom_call", output_to_operand_aliasing={{2}: (11, {}), {3}: (12, {}), {4}: (13, {})} | custom-call | flops 10616832000 | bytes 18874368 | tf_op jit(solution)/shard_map/exterior/pallas_call | solution.py:452
  46.5 1.8 %collective-permute-start.5 = (bf16[4,17,8,256]{3,2,1,0:T(8,128)(2,1)S(1)}, bf16[4,17,8,256]{3,2,1,0:T(8,128)(2,1)S(1)}, u32[]{:S(2)}, u32[]{:S(2)}) collective-permute-start(bf16[4,17,8,256]{3,2,1,0:T(8,128)(2,1)S(1)} %get-tuple-element.40), channel_id=1, source_target_pairs={{0,128},{128,0},{1,129},{129,1},{2,130},{130,2},{3,131},{131,3},{4... | collective-permute-start | bytes 835592 | tf_op jit(solution)/shard_map/ppermute | solution.py:467
  48.3 1.2 %collective-permute-done.5.got = bf16[4,17,8,256]{3,2,1,0:T(8,128)(2,1)S(1)} collective-permute-done((bf16[4,17,8,256]{3,2,1,0:T(8,128)(2,1)S(1)}, bf16[4,17,8,256]{3,2,1,0:T(8,128)(2,1)S(1)}, u32[]{:S(2)}, u32[]{:S(2)}) %collective-permute-start.5) | collective-permute-done | bytes 278560 | tf_op jit(solution)/shard_map/ppermute | solution.py:467
  49.5 0.8 %merge.1 = bf16[4,34,8,256]{3,2,1,0:T(8,128)(2,1)} custom-call(bf16[4,17,8,256]{3,2,1,0:T(8,128)(2,1)S(1)} %get-tuple-element.39.mine, bf16[4,17,8,256]{3,2,1,0:T(8,128)(2,1)S(1)} %collective-permute-done.5.got), custom_call_target="tpu_custom_call" | custom-call | tf_op jit(solution)/shard_map/merge/pallas_call | solution.py:468
Async XLA Ops:
  0.0 10.2 %collective-permute-start = (bf16[4,34,8,256]{3,2,1,0:T(8,128)(2,1)}, bf16[4,34,8,256]{3,2,1,0:T(8,128)(2,1)S(1)}, u32[]{:S(2)}, u32[]{:S(2)}) collective-permute-start(bf16[4,34,8,256]{3,2,1,0:T(8,128)(2,1)} %latent.1), channel_id=1, source_target_pairs={{0,128},{128,0},{1,129},{129,1},{2,130},{130,2},{3,131},{131,3},{4... | collective-permute-start | bytes 1671176 | tf_op jit(solution)/shard_map/ppermute | solution.py:395
  2.0 8.2 %collective-permute-start.1 = (bf16[10,3,8,256]{3,2,1,0:T(8,128)(2,1)S(1)}, bf16[10,3,8,256]{3,2,1,0:T(8,128)(2,1)S(1)}, u32[]{:S(2)}, u32[]{:S(2)}) collective-permute-start(bf16[10,3,8,256]{3,2,1,0:T(8,128)(2,1)S(1)} %get-tuple-element.25), channel_id=1, source_target_pairs={{0,32},{32,64},{64,96},{160,128},{192,160},{224,192},{1,33},{33,65... | collective-permute-start | bytes 368648 | tf_op jit(solution)/shard_map/ppermute | solution.py:400
  4.1 6.1 %collective-permute-start.2 = (bf16[4,3,8,256]{3,2,1,0:T(8,128)(2,1)S(1)}, bf16[4,3,8,256]{3,2,1,0:T(8,128)(2,1)S(1)}, u32[]{:S(2)}, u32[]{:S(2)}) collective-permute-start(bf16[4,3,8,256]{3,2,1,0:T(8,128)(2,1)S(1)} %get-tuple-element.26), channel_id=1, source_target_pairs={{128,32},{160,64},{192,96},{32,128},{64,160},{96,192},{129,33},{16... | collective-permute-start | bytes 147464 | tf_op jit(solution)/shard_map/ppermute | solution.py:401
  10.1 7.5 %copy-start = (bf16[2,34,8,256]{3,2,1,0:T(8,128)(2,1)S(1)}, bf16[2,34,8,256]{3,2,1,0:T(8,128)(2,1)}, u32[]{:S(2)}) copy-start(bf16[2,34,8,256]{3,2,1,0:T(8,128)(2,1)} %key_cache.1) | copy-start | bytes 835588
  10.1 7.4 %copy-start.1 = (bf16[2,34,8,256]{3,2,1,0:T(8,128)(2,1)S(1)}, bf16[2,34,8,256]{3,2,1,0:T(8,128)(2,1)}, u32[]{:S(2)}) copy-start(bf16[2,34,8,256]{3,2,1,0:T(8,128)(2,1)} %value_cache.1) | copy-start | bytes 835588
  10.1 7.4 %copy-start.2 = (bf16[256,256]{1,0:T(8,128)(2,1)S(1)}, bf16[256,256]{1,0:T(8,128)(2,1)}, u32[]{:S(2)}) copy-start(bf16[256,256]{1,0:T(8,128)(2,1)} %wq.3) | copy-start | bytes 393220
  10.1 7.4 %copy-start.3 = (bf16[256,256]{1,0:T(8,128)(2,1)S(1)}, bf16[256,256]{1,0:T(8,128)(2,1)}, u32[]{:S(2)}) copy-start(bf16[256,256]{1,0:T(8,128)(2,1)} %wk.3) | copy-start | bytes 393220
  10.2 7.4 %copy-start.4 = (bf16[256,256]{1,0:T(8,128)(2,1)S(1)}, bf16[256,256]{1,0:T(8,128)(2,1)}, u32[]{:S(2)}) copy-start(bf16[256,256]{1,0:T(8,128)(2,1)} %wv.3) | copy-start | bytes 393220
  10.2 7.4 %copy-start.5 = (bf16[256,256]{1,0:T(8,128)(2,1)S(1)}, bf16[256,256]{1,0:T(8,128)(2,1)}, u32[]{:S(2)}) copy-start(bf16[256,256]{1,0:T(8,128)(2,1)} %wo.3) | copy-start | bytes 393220
  10.2 7.4 %copy-start.6 = (f32[3,256]{1,0:T(4,128)S(1)}, f32[3,256]{1,0:T(4,128)}, u32[]{:S(2)}) copy-start(f32[3,256]{1,0:T(4,128)} %bias.3) | copy-start | bytes 9220
  11.2 16.3 %collective-permute-start.3 = (bf16[104,8,256]{2,1,0:T(8,128)(2,1)S(1)}, bf16[104,8,256]{2,1,0:T(8,128)(2,1)S(1)}, u32[]{:S(2)}, u32[]{:S(2)}) collective-permute-start(bf16[104,8,256]{2,1,0:T(8,128)(2,1)S(1)} %get-tuple-element.29), channel_id=1, source_target_pairs={{0,1},{1,2},{2,3},{3,4},{4,5},{5,6},{6,7},{7,8},{8,9},{9,10},{10,1... | collective-permute-start | bytes 1277960 | tf_op jit(solution)/shard_map/ppermute | solution.py:431
  15.6 15.7 %collective-permute-start.4 = (bf16[104,8,256]{2,1,0:T(8,128)(2,1)S(1)}, bf16[104,8,256]{2,1,0:T(8,128)(2,1)S(1)}, u32[]{:S(2)}, u32[]{:S(2)}) collective-permute-start(bf16[104,8,256]{2,1,0:T(8,128)(2,1)S(1)} %get-tuple-element.30), channel_id=1, source_target_pairs={{1,0},{2,1},{3,2},{4,3},{5,4},{6,5},{7,6},{8,7},{9,8},{10,9},{11,1... | collective-permute-start | bytes 1277960 | tf_op jit(solution)/shard_map/ppermute | solution.py:430
  46.5 3.0 %collective-permute-start.5 = (bf16[4,17,8,256]{3,2,1,0:T(8,128)(2,1)S(1)}, bf16[4,17,8,256]{3,2,1,0:T(8,128)(2,1)S(1)}, u32[]{:S(2)}, u32[]{:S(2)}) collective-permute-start(bf16[4,17,8,256]{3,2,1,0:T(8,128)(2,1)S(1)} %get-tuple-element.40), channel_id=1, source_target_pairs={{0,128},{128,0},{1,129},{129,1},{2,130},{130,2},{3,131},{131,3},{4... | collective-permute-start | bytes 835592 | tf_op jit(solution)/shard_map/ppermute | solution.py:467
